TPU v7x, 32 devices: a whole 2x2x4 slice. The times are simulated.
32 devices in a mesh: tlo: 2 (over y), thi: 16 (over z, x, core).
Axes of the slice: x: 2, y: 2, z: 4, core: 2. Of those that a mesh axis runs over, the one named last changes fastest.
Arguments:
- frames_in: bfloat16 [4, 4096, 384], P(None, ('thi', 'tlo')), may hold values from -6 to 6
- weights: bfloat16 [4, 3, 384, 384], replicated, may hold values from -0.1875 to 0.1875
- biases: float32 [4, 384], replicated, may hold values from -3 to 3
- valid_mask: int32 [4, 4096], P(None, ('thi', 'tlo')), may hold values 0 or 1
- cotangent: bfloat16 [4, 4096, 384], P(None, ('thi', 'tlo')), may hold values from -6 to 6
Outputs:
- input_grad: bfloat16 [4, 4096, 384], P(None, ('thi', 'tlo'))
- weight_grad: float32 [4, 3, 384, 384], replicated
- bias_grad: float32 [4, 384], replicated
All inputs are finite; a program needn't handle non-finite values. No bound on the sum of `valid_mask` on one device may be relied on, other than what follows from the above.
Results may differ from a plain program's by a relative error of at most 0.015.
Values may be sent and summed in bfloat16 or wider, within the bound.
A program may use at most 128 MiB of HBM per device.

v0:
```python
import math

import jax
import jax.numpy as jnp
from jax import lax
from jax.sharding import PartitionSpec as P


def shifted(block, axis, distance):
    devices = range(lax.axis_size(axis))
    route = [((i - distance) % len(devices), i) for i in devices]
    return lax.ppermute(block, axis, route)


def from_behind(value, axis, steps):
    count = lax.axis_size(axis)
    first, last = (max(0, -steps), min(count, count - steps))
    return lax.ppermute(value, axis, [(source, source + steps) for source in range(first, last)])


def smooth(values):
    return jax.nn.gelu(values, approximate=True)


def shift_shards(values, count):
    inner_size = lax.axis_size("tlo")
    outer_size = lax.axis_size("thi")
    if abs(count) >= inner_size * outer_size:
        return jnp.zeros_like(values)
    outer_by, inner_by = divmod(count, inner_size)
    rolled = values if inner_by == 0 else shifted(values, "tlo", inner_by)
    nearer = rolled if outer_by == 0 else from_behind(rolled, "thi", outer_by)
    if inner_by == 0:
        return nearer
    farther = rolled if outer_by + 1 == 0 else from_behind(rolled, "thi", outer_by + 1)
    return jnp.where(lax.axis_index("tlo") < inner_by, farther, nearer)


def tap_pair(values, dilation, sign):
    frames_dev = values.shape[1]
    if dilation < frames_dev:
        if sign > 0:
            edge = shift_shards(values[:, frames_dev - 2 * dilation :, :], 1)
            joined = jnp.concatenate([edge, values], axis=1)
            return (joined[:, dilation : dilation + frames_dev], joined[:, :frames_dev])
        edge = shift_shards(values[:, : 2 * dilation, :], -1)
        joined = jnp.concatenate([values, edge], axis=1)
        return (
            joined[:, dilation : dilation + frames_dev],
            joined[:, 2 * dilation : 2 * dilation + frames_dev],
        )
    hop_count = sign * (dilation // frames_dev)
    first = shift_shards(values, hop_count)
    second = shift_shards(values, 2 * hop_count)
    return (first, second)


def reduce_grads(weight_part, bias_part):
    return lax.psum((weight_part, bias_part), ("tlo", "thi"))


def shards(frames_in, weights, biases, valid_mask, cotangent):
    windows, frames_dev, channels = frames_in.shape
    widths = 3 * channels
    levels = weights.shape[0]
    keep = valid_mask.astype(jnp.float32)[:, :, None]
    dilations = [frames_dev // 4, frames_dev, 8 * frames_dev, 32 * frames_dev]
    current = frames_in
    saved = []
    for level in range(levels):
        first, second = tap_pair(current, dilations[level], 1)
        stacked = jnp.concatenate([current, first, second], axis=2).reshape(
            windows * frames_dev, widths
        )
        pre = (
            jnp.dot(
                stacked,
                weights[level].reshape(widths, channels),
                preferred_element_type=jnp.float32,
            )
            + biases[level]
        )
        pre = pre.reshape(windows, frames_dev, channels)
        current = (keep * (current.astype(jnp.float32) + smooth(pre))).astype(jnp.bfloat16)
        saved.append((stacked, pre))
    upstream = cotangent
    pending_weight = [None] * levels
    pending_bias = [None] * levels
    for level in reversed(range(levels)):
        stacked, pre = saved[level]
        through = upstream.astype(jnp.float32) * keep
        pull = jax.vjp(smooth, pre)[1]
        pre_grad = pull(through)[0].astype(jnp.bfloat16)
        flat_grad = pre_grad.reshape(windows * frames_dev, channels)
        weight_part = jnp.einsum(
            "rk,rc->kc", stacked, flat_grad, preferred_element_type=jnp.float32
        )
        bias_part = jnp.sum(flat_grad.astype(jnp.float32), axis=0)
        pending_weight[level] = weight_part
        pending_bias[level] = bias_part
        first, second = tap_pair(pre_grad, dilations[level], -1)
        gathered = jnp.concatenate([pre_grad, first, second], axis=2).reshape(
            windows * frames_dev, widths
        )
        mirrored = jnp.transpose(weights[level], (0, 2, 1)).reshape(widths, channels)
        back = jnp.dot(gathered, mirrored, preferred_element_type=jnp.float32).reshape(
            windows, frames_dev, channels
        )
        upstream = (through + back).astype(jnp.bfloat16)
    totals = reduce_grads(jnp.stack(pending_weight), jnp.stack(pending_bias))
    weight_sum = totals[0]
    bias_sum = totals[1]
    factor = 1.0 / math.sqrt(windows * frames_dev * lax.axis_size("tlo") * lax.axis_size("thi"))
    weight_grad = (weight_sum * factor).reshape(levels, 3, channels, channels)
    bias_grad = bias_sum * factor
    return (upstream, weight_grad, bias_grad)


def solution(mesh):
    return jax.shard_map(
        shards,
        mesh=mesh,
        in_specs=(
            P(None, ("thi", "tlo"), None),
            P(),
            P(),
            P(None, ("thi", "tlo")),
            P(None, ("thi", "tlo"), None),
        ),
        out_specs=(P(None, ("thi", "tlo"), None), P(), P()),
        check_vma=False,
    )
```

profile of v0, /device:TPU:1, one launch (start us, length us, event | category | flops | bytes accessed | tf_op | source)
XLA Modules:
  0.0 335.3 jit_solution(8208116632094530155)
XLA Ops:
  7.2 1.0 slice.46
  8.2 2.1 collective-permute-start
  10.3 4.6 %collective-permute-done = bf16[4,64,384]{2,1,0:T(8,128)(2,1)S(1)} collective-permute-done((bf16[4,64,384]{2,1,0:T(8,128)(2,1)S(1)}, bf16[4,64,384]{2,1,0:T(8,128)(2,1)S(1)}, u32[]{:S(2)}, u32[]{:S(2)}) %collective-permute-start) | collective-permute-done | bytes 196640 | tf_op jit(solution)/shard_map/ppermute | solution.py:12
  15.0 4.4 %collective-permute-start.1 = (bf16[4,64,384]{2,1,0:T(8,128)(2,1)S(1)}, bf16[4,64,384]{2,1,0:T(8,128)(2,1)S(1)}, u32[]{:S(2)}, u32[]{:S(2)}) collective-permute-start(bf16[4,64,384]{2,1,0:T(8,128)(2,1)S(1)} %collective-permute-done), channel_id=1, source_target_pairs={{0,1},{1,2},{2,3},{3,4},{4,5},{5,6},{6,7},{7,8},{8,9},{9,10},{10,1... | collective-permute-start | bytes 589832 | tf_op jit(solution)/shard_map/ppermute | solution.py:18
  19.4 4.8 %slice_bitcast_fusion.3 = (bf16[3,384,384]{1,2,0:T(8,128)(2,1)S(1)}, bf16[3,384,384]{1,2,0:T(8,128)(2,1)}, bf16[3,384,384]{1,2,0:T(8,128)(2,1)}, bf16[3,384,384]...) fusion(bf16[4,3,384,384]{3,2,1,0:T(8,128)(2,1)} %param.6), kind=kLoop, calls=%fused_computation.114 | loop fusion | bytes 10616832 | tf_op jit(solution)/shard_map/transpose | solution.py:105
  24.2 0.2 copy.20
  24.5 0.2 copy.18
  24.8 0.3 fusion.57
  25.1 0.8 copy-done.3
  25.8 0.2 fusion.13
  26.1 1.4 copy.21
  27.5 2.3 convolution_add_fusion.7
  29.8 0.3 multiply_convert_fusion.2
  30.1 1.3 collective-permute-start.2
  31.4 8.1 %collective-permute-done.2 = bf16[4,128,384]{2,1,0:T(8,128)(2,1)S(1)} collective-permute-done((bf16[4,128,384]{2,1,0:T(8,128)(2,1)S(1)}, bf16[4,128,384]{2,1,0:T(8,128)(2,1)S(1)}, u32[]{:S(2)}, u32[]{:S(2)}) %collective-permute-start.2) | collective-permute-done | bytes 393248 | tf_op jit(solution)/shard_map/ppermute | solution.py:12
  39.6 3.9 %collective-permute-start.3 = (bf16[4,128,384]{2,1,0:T(8,128)(2,1)S(1)}, bf16[4,128,384]{2,1,0:T(8,128)(2,1)S(1)}, u32[]{:S(2)}, u32[]{:S(2)}) collective-permute-start(bf16[4,128,384]{2,1,0:T(8,128)(2,1)S(1)} %collective-permute-done.2), channel_id=1, source_target_pairs={{0,1},{1,2},{2,3},{3,4},{4,5},{5,6},{6,7},{7,8},{8,9},{9,10},{10,1... | collective-permute-start | bytes 1179656 | tf_op jit(solution)/shard_map/ppermute | solution.py:18
  43.5 2.4 collective-permute-start.4
  45.9 2.3 collective-permute-done.3
  48.2 4.2 %collective-permute-done.4 = bf16[4,128,384]{2,1,0:T(8,128)(2,1)S(1)} collective-permute-done((bf16[4,128,384]{2,1,0:T(8,128)(2,1)S(1)}, bf16[4,128,384]{2,1,0:T(8,128)(2,1)S(1)}, u32[]{:S(2)}, u32[]{:S(2)}) %collective-permute-start.4) | collective-permute-done | bytes 393248 | tf_op jit(solution)/shard_map/ppermute | solution.py:18
  52.4 0.1 pad_maximum_fusion.3
  52.5 0.8 convolution_add_fusion.6
  53.4 0.9 copy-done.1
  54.3 1.4 multiply_convert_fusion.1
  55.6 4.9 %collective-permute-start.6 = (bf16[4,128,384]{2,1,0:T(8,128)(2,1)}, bf16[4,128,384]{2,1,0:T(8,128)(2,1)}, u32[]{:S(2)}, u32[]{:S(2)}) collective-permute-start(bf16[4,128,384]{2,1,0:T(8,128)(2,1)} %multiply_convert_fusion.1), channel_id=1, source_target_pairs={{0,8},{1,9},{2,10},{3,11},{4,12},{5,13},{6,14},{7,15},{16,24},{17,... | collective-permute-start | bytes 1179656 | tf_op jit(solution)/shard_map/ppermute | solution.py:18
  60.6 3.5 %collective-permute-start.5 = (bf16[4,128,384]{2,1,0:T(8,128)(2,1)}, bf16[4,128,384]{2,1,0:T(8,128)(2,1)}, u32[]{:S(2)}, u32[]{:S(2)}) collective-permute-start(bf16[4,128,384]{2,1,0:T(8,128)(2,1)} %multiply_convert_fusion.1), channel_id=1, source_target_pairs={{0,4},{1,5},{2,6},{3,7},{4,8},{5,9},{6,10},{7,11},{8,12},{9,13},{1... | collective-permute-start | bytes 1179656 | tf_op jit(solution)/shard_map/ppermute | solution.py:18
  64.1 2.3 copy.22
  66.4 7.1 %collective-permute-done.5 = bf16[4,128,384]{2,1,0:T(8,128)(2,1)} collective-permute-done((bf16[4,128,384]{2,1,0:T(8,128)(2,1)}, bf16[4,128,384]{2,1,0:T(8,128)(2,1)}, u32[]{:S(2)}, u32[]{:S(2)}) %collective-permute-start.5) | collective-permute-done | bytes 393248 | tf_op jit(solution)/shard_map/ppermute | solution.py:18
  73.5 1.3 pad_maximum_fusion.4
  74.9 0.8 convolution_add_fusion.5
  75.7 0.3 copy-done.2
  76.0 0.9 multiply_convert_fusion
  76.9 0.1 concatenate.34
  77.0 0.2 copy-done.13
  77.1 0.8 convolution_add_fusion.4
  78.0 0.1 copy-done.18
  78.1 0.6 convert_reduce_fusion
  78.7 2.2 convert_reduce_fusion.1
  80.9 1.3 collective-permute-start.8
  82.2 1.5 collective-permute-start.7
  83.7 2.3 copy.23
  85.9 28.3 %collective-permute-done.8 = bf16[4,128,384]{2,1,0:T(8,128)(2,1)} collective-permute-done((bf16[4,128,384]{2,1,0:T(8,128)(2,1)S(1)}, bf16[4,128,384]{2,1,0:T(8,128)(2,1)}, u32[]{:S(2)}, u32[]{:S(2)}) %collective-permute-start.8) | collective-permute-done | bytes 393248 | tf_op jit(solution)/shard_map/ppermute | solution.py:18
  114.2 4.1 %convert_reduce_fusion.2 = (f32[384]{0:T(512)S(1)}, bf16[4,128,384]{2,1,0:T(8,128)(2,1)}, f32[4,128,384]{2,1,0:T(8,128)}) fusion(f32[4,128,384]{2,1,0:T(8,128)} %bitcast.81, f32[4,128]{1,0:T(4,128)S(1)} %convert_element_type.74, f32[4,128,384]{2,1,0:T(8,128)} %get-tuple-element.23, bf16[1152,384,1]{1,0,2:T(8,128)(2,1)} %bitcast.89, ...), kind=kOutput, calls=%fused_computation.85 | convolution fusion | flops 461635200 | bytes 4820480 | tf_op jit(solution)/shard_map/dot_general | solution.py:106
  118.4 1.2 collective-permute-start.9
  119.6 2.3 copy.24
  121.9 1.8 convolution_bitcast_fusion
  123.7 3.4 %collective-permute-done.9 = bf16[4,128,384]{2,1,0:T(8,128)(2,1)} collective-permute-done((bf16[4,128,384]{2,1,0:T(8,128)(2,1)}, bf16[4,128,384]{2,1,0:T(8,128)(2,1)}, u32[]{:S(2)}, u32[]{:S(2)}) %collective-permute-start.9) | collective-permute-done | bytes 393248 | tf_op jit(solution)/shard_map/ppermute | solution.py:12
  127.1 5.0 %collective-permute-start.10 = (bf16[4,128,384]{2,1,0:T(8,128)(2,1)}, bf16[4,128,384]{2,1,0:T(8,128)(2,1)S(1)}, u32[]{:S(2)}, u32[]{:S(2)}) collective-permute-start(bf16[4,128,384]{2,1,0:T(8,128)(2,1)} %collective-permute-done.9), channel_id=1, source_target_pairs={{1,0},{2,1},{3,2},{4,3},{5,4},{6,5},{7,6},{8,7},{9,8},{10,9},{11,1... | collective-permute-start | bytes 1179656 | tf_op jit(solution)/shard_map/ppermute | solution.py:18
  132.1 2.0 convolution_bitcast_fusion.1
  134.2 2.1 collective-permute-start.11
  136.3 1.8 convolution_bitcast_fusion.2
  138.1 1.1 broadcast_select_fusion
  139.2 4.5 %collective-permute-done.11 = bf16[4,128,384]{2,1,0:T(8,128)(2,1)S(1)} collective-permute-done((bf16[4,128,384]{2,1,0:T(8,128)(2,1)}, bf16[4,128,384]{2,1,0:T(8,128)(2,1)S(1)}, u32[]{:S(2)}, u32[]{:S(2)}) %collective-permute-start.11) | collective-permute-done | bytes 393248 | tf_op jit(solution)/shard_map/ppermute | solution.py:18
  143.6 3.2 convert_reduce_fusion.3
  146.8 0.8 convolution_bitcast_fusion.3
  147.6 3.2 pad_maximum_fusion
  150.9 1.3 collective-permute-start.12
  152.2 2.3 copy.25
  154.6 46.6 %psum.15 = f32[4,384]{1,0:T(4,128)S(1)} all-reduce(f32[4,384]{1,0:T(4,128)S(1)} %pad_maximum_fusion.5), channel_id=1, replica_groups=mesh['tlo'=2,'thi'=16] {'tlo','thi'}, use_global_device_ids=true, to_apply=%region_5.6 | all-reduce | flops 1536 | bytes 12288 | tf_op jit(solution)/shard_map/psum | solution.py:59
  201.1 3.0 collective-permute-start.13
  204.1 0.6 broadcast_multiply_fusion.1
  204.7 9.0 %collective-permute-done.13 = bf16[4,64,384]{2,1,0:T(8,128)(2,1)S(1)} collective-permute-done((bf16[4,64,384]{2,1,0:T(8,128)(2,1)S(1)}, bf16[4,64,384]{2,1,0:T(8,128)(2,1)S(1)}, u32[]{:S(2)}, u32[]{:S(2)}) %collective-permute-start.13) | collective-permute-done | bytes 196640 | tf_op jit(solution)/shard_map/ppermute | solution.py:18
  213.9 2.7 fusion.3
  216.5 105.5 %all-reduce.4.cloned.1.call-done = f32[4,1152,384]{2,1,0:T(8,128)} async-done(((f32[4,1152,384]{2,1,0:T(8,128)}), f32[4,1152,384]{2,1,0:T(8,128)}) %all-reduce.4.cloned.1.call-update) | async-done | bytes 7077904 | tf_op jit(solution)/shard_map/psum | solution.py:59
  322.0 6.4 %broadcast_multiply_fusion = f32[4,1152,384]{2,1,0:T(8,128)} fusion(f32[4,1152,384]{2,1,0:T(8,128)} %all-reduce.4.cloned.1.call-done), kind=kLoop, calls=%fused_computation.1 | loop fusion | flops 1769472 | bytes 14155776 | tf_op jit(solution)/shard_map/mul | solution.py:114
  (64 shorter events, 0.4 us)
Async XLA Ops:
  7.2 314.8 %all-reduce.4.cloned.1.call-start = ((), (), s32[]{:S(2)}) async-start(), calls=%async_computation | async-start | bytes 14155776 | tf_op jit(solution)/shard_map/psum | solution.py:59
  8.2 16.0 %copy-start = (bf16[4,128,384]{2,1,0:T(8,128)(2,1)S(1)}, bf16[4,128,384]{2,1,0:T(8,128)(2,1)}, u32[]{:S(2)}) copy-start(bf16[4,128,384]{2,1,0:T(8,128)(2,1)} %param.5) | copy-start | bytes 1179652
  8.2 16.2 %copy-start.21 = (s32[4,128]{1,0:T(4,128)S(1)}, s32[4,128]{1,0:T(4,128)}, u32[]{:S(2)}) copy-start(s32[4,128]{1,0:T(4,128)} %param.8) | copy-start | bytes 6148
  8.2 16.3 %copy-start.20 = (f32[4,384]{1,0:T(4,128)S(1)}, f32[4,384]{1,0:T(4,128)}, u32[]{:S(2)}) copy-start(f32[4,384]{1,0:T(4,128)} %param.7) | copy-start | bytes 18436
  8.2 6.8 %collective-permute-start = (bf16[4,64,384]{2,1,0:T(8,128)(2,1)S(1)}, bf16[4,64,384]{2,1,0:T(8,128)(2,1)S(1)}, u32[]{:S(2)}, u32[]{:S(2)}) collective-permute-start(bf16[4,64,384]{2,1,0:T(8,128)(2,1)S(1)} %slice.46), channel_id=1, source_target_pairs={{16,0},{0,16},{17,1},{1,17},{18,2},{2,18},{19,3},{3,19},{20,4},{4,... | collective-permute-start | bytes 589832 | tf_op jit(solution)/shard_map/ppermute | solution.py:12
  15.0 9.5 %collective-permute-start.1 = (bf16[4,64,384]{2,1,0:T(8,128)(2,1)S(1)}, bf16[4,64,384]{2,1,0:T(8,128)(2,1)S(1)}, u32[]{:S(2)}, u32[]{:S(2)}) collective-permute-start(bf16[4,64,384]{2,1,0:T(8,128)(2,1)S(1)} %collective-permute-done), channel_id=1, source_target_pairs={{0,1},{1,2},{2,3},{3,4},{4,5},{5,6},{6,7},{7,8},{8,9},{9,10},{10,1... | collective-permute-start | bytes 589832 | tf_op jit(solution)/shard_map/ppermute | solution.py:18
  25.1 0.8 copy-start.3
  30.1 22.4 %copy-start.15 = (bf16[1,3,384,384]{3,2,1,0:T(8,128)(2,1)S(1)}, bf16[1,3,384,384]{3,2,1,0:T(8,128)(2,1)}, u32[]{:S(2)}) copy-start(bf16[1,3,384,384]{3,2,1,0:T(8,128)(2,1)} %get-tuple-element.19) | copy-start | bytes 2654212
  30.1 9.4 %collective-permute-start.2 = (bf16[4,128,384]{2,1,0:T(8,128)(2,1)S(1)}, bf16[4,128,384]{2,1,0:T(8,128)(2,1)S(1)}, u32[]{:S(2)}, u32[]{:S(2)}) collective-permute-start(bf16[4,128,384]{2,1,0:T(8,128)(2,1)S(1)} %multiply_convert_fusion.2), channel_id=1, source_target_pairs={{16,0},{0,16},{17,1},{1,17},{18,2},{2,18},{19,3},{3,19},{20,4},{4,... | collective-permute-start | bytes 1179656 | tf_op jit(solution)/shard_map/ppermute | solution.py:12
  39.6 8.6 %collective-permute-start.3 = (bf16[4,128,384]{2,1,0:T(8,128)(2,1)S(1)}, bf16[4,128,384]{2,1,0:T(8,128)(2,1)S(1)}, u32[]{:S(2)}, u32[]{:S(2)}) collective-permute-start(bf16[4,128,384]{2,1,0:T(8,128)(2,1)S(1)} %collective-permute-done.2), channel_id=1, source_target_pairs={{0,1},{1,2},{2,3},{3,4},{4,5},{5,6},{6,7},{7,8},{8,9},{9,10},{10,1... | collective-permute-start | bytes 1179656 | tf_op jit(solution)/shard_map/ppermute | solution.py:18
  43.5 8.9 %collective-permute-start.4 = (bf16[4,128,384]{2,1,0:T(8,128)(2,1)S(1)}, bf16[4,128,384]{2,1,0:T(8,128)(2,1)S(1)}, u32[]{:S(2)}, u32[]{:S(2)}) collective-permute-start(bf16[4,128,384]{2,1,0:T(8,128)(2,1)S(1)} %multiply_convert_fusion.2), channel_id=1, source_target_pairs={{0,1},{1,2},{2,3},{3,4},{4,5},{5,6},{6,7},{7,8},{8,9},{9,10},{10,1... | collective-permute-start | bytes 1179656 | tf_op jit(solution)/shard_map/ppermute | solution.py:18
  48.2 5.1 %copy-start.5 = (bf16[4,128,384]{2,1,0:T(8,128)(2,1)}, bf16[4,128,384]{2,1,0:T(8,128)(2,1)S(1)}, u32[]{:S(2)}) copy-start(bf16[4,128,384]{2,1,0:T(8,128)(2,1)S(1)} %broadcast_select_fusion.1) | copy-start | bytes 1179652
  52.4 1.0 copy-start.16
  53.4 0.9 copy-start.1
  55.6 10.7 %collective-permute-start.6 = (bf16[4,128,384]{2,1,0:T(8,128)(2,1)}, bf16[4,128,384]{2,1,0:T(8,128)(2,1)}, u32[]{:S(2)}, u32[]{:S(2)}) collective-permute-start(bf16[4,128,384]{2,1,0:T(8,128)(2,1)} %multiply_convert_fusion.1), channel_id=1, source_target_pairs={{0,8},{1,9},{2,10},{3,11},{4,12},{5,13},{6,14},{7,15},{16,24},{17,... | collective-permute-start | bytes 1179656 | tf_op jit(solution)/shard_map/ppermute | solution.py:18
  60.6 12.9 %collective-permute-start.5 = (bf16[4,128,384]{2,1,0:T(8,128)(2,1)}, bf16[4,128,384]{2,1,0:T(8,128)(2,1)}, u32[]{:S(2)}, u32[]{:S(2)}) collective-permute-start(bf16[4,128,384]{2,1,0:T(8,128)(2,1)} %multiply_convert_fusion.1), channel_id=1, source_target_pairs={{0,4},{1,5},{2,6},{3,7},{4,8},{5,9},{6,10},{7,11},{8,12},{9,13},{1... | collective-permute-start | bytes 1179656 | tf_op jit(solution)/shard_map/ppermute | solution.py:18
  66.4 8.5 %copy-start.14 = (bf16[1,3,384,384]{3,2,1,0:T(8,128)(2,1)S(1)}, bf16[1,3,384,384]{3,2,1,0:T(8,128)(2,1)}, u32[]{:S(2)}) copy-start(bf16[1,3,384,384]{3,2,1,0:T(8,128)(2,1)} %get-tuple-element.22) | copy-start | bytes 2654212
  74.8 1.1 copy-start.2
  76.0 1.2 copy-start.13
  76.9 1.1 copy-start.7
  77.0 1.1 copy-start.18
  77.1 1.6 copy-start.10
  78.7 2.2 copy-start.19
  80.9 33.3 %copy-start.22 = (bf16[4,128,384]{2,1,0:T(8,128)(2,1)}, bf16[4,128,384]{2,1,0:T(8,128)(2,1)S(1)}, u32[]{:S(2)}) copy-start(bf16[4,128,384]{2,1,0:T(8,128)(2,1)S(1)} %get-tuple-element.12) | copy-start | bytes 1179652
  80.9 33.3 %collective-permute-start.8 = (bf16[4,128,384]{2,1,0:T(8,128)(2,1)S(1)}, bf16[4,128,384]{2,1,0:T(8,128)(2,1)}, u32[]{:S(2)}, u32[]{:S(2)}) collective-permute-start(bf16[4,128,384]{2,1,0:T(8,128)(2,1)S(1)} %get-tuple-element.12), channel_id=1, source_target_pairs={{8,0},{9,1},{10,2},{11,3},{12,4},{13,5},{14,6},{15,7},{24,16},{25,... | collective-permute-start | bytes 1179656 | tf_op jit(solution)/shard_map/ppermute | solution.py:18
  82.2 32.0 %collective-permute-start.7 = (bf16[4,128,384]{2,1,0:T(8,128)(2,1)S(1)}, bf16[4,128,384]{2,1,0:T(8,128)(2,1)}, u32[]{:S(2)}, u32[]{:S(2)}) collective-permute-start(bf16[4,128,384]{2,1,0:T(8,128)(2,1)S(1)} %get-tuple-element.12), channel_id=1, source_target_pairs={{4,0},{5,1},{6,2},{7,3},{8,4},{9,5},{10,6},{11,7},{12,8},{13,9},{1... | collective-permute-start | bytes 1179656 | tf_op jit(solution)/shard_map/ppermute | solution.py:18
  118.4 3.5 %copy-start.8 = (bf16[4,128,384]{2,1,0:T(8,128)(2,1)S(1)}, bf16[4,128,384]{2,1,0:T(8,128)(2,1)}, u32[]{:S(2)}) copy-start(bf16[4,128,384]{2,1,0:T(8,128)(2,1)} %copy-done.7) | copy-start | bytes 1179652
  118.4 8.8 %collective-permute-start.9 = (bf16[4,128,384]{2,1,0:T(8,128)(2,1)}, bf16[4,128,384]{2,1,0:T(8,128)(2,1)}, u32[]{:S(2)}, u32[]{:S(2)}) collective-permute-start(bf16[4,128,384]{2,1,0:T(8,128)(2,1)} %get-tuple-element.10), channel_id=1, source_target_pairs={{16,0},{0,16},{17,1},{1,17},{18,2},{2,18},{19,3},{3,19},{20,4},{4,... | collective-permute-start | bytes 1179656 | tf_op jit(solution)/shard_map/ppermute | solution.py:12
  121.9 10.3 %copy-start.23 = (bf16[4,128,384]{2,1,0:T(8,128)(2,1)S(1)}, bf16[4,128,384]{2,1,0:T(8,128)(2,1)}, u32[]{:S(2)}) copy-start(bf16[4,128,384]{2,1,0:T(8,128)(2,1)} %copy-done.22) | copy-start | bytes 1179652
  123.7 12.6 %copy-start.6 = (bf16[4,128,384]{2,1,0:T(8,128)(2,1)S(1)}, bf16[4,128,384]{2,1,0:T(8,128)(2,1)}, u32[]{:S(2)}) copy-start(bf16[4,128,384]{2,1,0:T(8,128)(2,1)} %copy-done.5) | copy-start | bytes 1179652
  123.7 12.6 %copy-start.17 = (bf16[4,128,384]{2,1,0:T(8,128)(2,1)S(1)}, bf16[4,128,384]{2,1,0:T(8,128)(2,1)}, u32[]{:S(2)}) copy-start(bf16[4,128,384]{2,1,0:T(8,128)(2,1)} %copy-done.16) | copy-start | bytes 1179652
  127.1 10.9 %collective-permute-start.10 = (bf16[4,128,384]{2,1,0:T(8,128)(2,1)}, bf16[4,128,384]{2,1,0:T(8,128)(2,1)S(1)}, u32[]{:S(2)}, u32[]{:S(2)}) collective-permute-start(bf16[4,128,384]{2,1,0:T(8,128)(2,1)} %collective-permute-done.9), channel_id=1, source_target_pairs={{1,0},{2,1},{3,2},{4,3},{5,4},{6,5},{7,6},{8,7},{9,8},{10,9},{11,1... | collective-permute-start | bytes 1179656 | tf_op jit(solution)/shard_map/ppermute | solution.py:18
  134.2 9.5 %copy-start.9 = (bf16[3,384,384]{2,1,0:T(8,128)(2,1)S(1)}, bf16[3,384,384]{2,1,0:T(8,128)(2,1)}, u32[]{:S(2)}) copy-start(bf16[3,384,384]{2,1,0:T(8,128)(2,1)} %copy.24) | copy-start | bytes 2654212
  134.2 9.5 %copy-start.24 = (f32[4,128,384]{2,1,0:T(8,128)S(1)}, f32[4,128,384]{2,1,0:T(8,128)}, u32[]{:S(2)}) copy-start(f32[4,128,384]{2,1,0:T(8,128)} %get-tuple-element.24) | copy-start | bytes 2359300
  134.2 9.4 %collective-permute-start.11 = (bf16[4,128,384]{2,1,0:T(8,128)(2,1)}, bf16[4,128,384]{2,1,0:T(8,128)(2,1)S(1)}, u32[]{:S(2)}, u32[]{:S(2)}) collective-permute-start(bf16[4,128,384]{2,1,0:T(8,128)(2,1)} %get-tuple-element.10), channel_id=1, source_target_pairs={{1,0},{2,1},{3,2},{4,3},{5,4},{6,5},{7,6},{8,7},{9,8},{10,9},{11,1... | collective-permute-start | bytes 1179656 | tf_op jit(solution)/shard_map/ppermute | solution.py:18
  143.6 3.2 copy-start.4
  146.8 4.0 %copy-start.11 = (bf16[4,128,384]{2,1,0:T(8,128)(2,1)}, bf16[4,128,384]{2,1,0:T(8,128)(2,1)S(1)}, u32[]{:S(2)}) copy-start(bf16[4,128,384]{2,1,0:T(8,128)(2,1)S(1)} %get-tuple-element.8) | copy-start | bytes 1179652
  150.9 62.9 %copy-start.12 = (bf16[4,128,384]{2,1,0:T(8,128)(2,1)S(1)}, bf16[4,128,384]{2,1,0:T(8,128)(2,1)}, u32[]{:S(2)}) copy-start(bf16[4,128,384]{2,1,0:T(8,128)(2,1)} %copy-done.11) | copy-start | bytes 1179652
  150.9 50.2 %collective-permute-start.12 = (bf16[4,64,384]{2,1,0:T(8,128)(2,1)S(1)}, bf16[4,64,384]{2,1,0:T(8,128)(2,1)S(1)}, u32[]{:S(2)}, u32[]{:S(2)}) collective-permute-start(bf16[4,64,384]{2,1,0:T(8,128)(2,1)S(1)} %slice.62), channel_id=1, source_target_pairs={{16,0},{0,16},{17,1},{1,17},{18,2},{2,18},{19,3},{3,19},{20,4},{4,... | collective-permute-start | bytes 589832 | tf_op jit(solution)/shard_map/ppermute | solution.py:12
  201.1 12.6 %collective-permute-start.13 = (bf16[4,64,384]{2,1,0:T(8,128)(2,1)S(1)}, bf16[4,64,384]{2,1,0:T(8,128)(2,1)S(1)}, u32[]{:S(2)}, u32[]{:S(2)}) collective-permute-start(bf16[4,64,384]{2,1,0:T(8,128)(2,1)S(1)} %collective-permute-done.12), channel_id=1, source_target_pairs={{1,0},{2,1},{3,2},{4,3},{5,4},{6,5},{7,6},{8,7},{9,8},{10,9},{11,1... | collective-permute-start | bytes 589832 | tf_op jit(solution)/shard_map/ppermute | solution.py:18
Sparse Core Ops, SparseCore 0:
  151.0 170.9 all-reduce.3
where the time goes:
time: 337 us; the launch traced here: 335 us
  waiting for transfers between devices  177 us (53%)
  blocking collectives  46.6 us (14%)
  starting transfers between devices  37.9 us (11%)
  matrix products  23.3 us (7%)
  local copies, waits for them, and re-layouts  19.2 us (6%)
  other arithmetic  16.7 us (5%)
  between operations  14.6 us (4%)
    psum x1, waiting for transfers between devices, reduce_grads(): return lax.psum((weight_part, bias_part), ('tlo', 'thi'))  105 us
    ppermute x10, waiting for transfers between devices, from_behind(): lax.ppermute(value, axis, [(source, source + steps) for source in range(f...  55.4 us
    psum x1, blocking collectives, reduce_grads(): return lax.psum((weight_part, bias_part), ('tlo', 'thi'))  46.6 us
    ppermute x10, starting transfers between devices, from_behind(): lax.ppermute(value, axis, [(source, source + steps) for source in range(f...  31.9 us
    ppermute x4, waiting for transfers between devices, shifted(): return lax.ppermute(block, axis, route)  16.2 us
    transpose x5, local copies, waits for them, and re-layouts, shards(): jnp.transpose(weights[level], (0, 2, 1)).reshape(widths, channels)  13.9 us
    dot_general x4, matrix products, shards(): jnp.dot(gathered, mirrored, preferred_element_type=jnp.float32)  12.2 us
  transfers between devices with their start and end apart: 15, of which 10 were waited for; matrix products, arithmetic and copies ran while one was open for 7% of the time, Pallas kernels for 0%

commit v1 on v0

--- a/solution.py
+++ b/solution.py
@@ -3,7 +3,401 @@
 import jax
 import jax.numpy as jnp
 from jax import lax
+from jax.experimental import pallas as pl
+from jax.experimental.pallas import tpu as pltpu
 from jax.sharding import PartitionSpec as P
+
+MESH = pl.DeviceIdType.MESH
+F32 = jnp.float32
+BF16 = jnp.bfloat16
+UNITS = 4
+UNIT_ROWS = 1024
+
+
+def rows_times(a, b):
+    return jnp.dot(a, b, preferred_element_type=F32)
+
+
+def rows_times_t(a, b):
+    return lax.dot_general(a, b, (((1,), (1,)), ((), ())), preferred_element_type=F32)
+
+
+def t_times_rows(a, b):
+    return lax.dot_general(a, b, (((0,), (0,)), ((), ())), preferred_element_type=F32)
+
+
+def gelu_and_slope(v):
+    root = math.sqrt(2.0 / math.pi)
+    square = v * v
+    t = jnp.tanh(root * (v + 0.044715 * (square * v)))
+    half = 0.5 * (1.0 + t)
+    slope = half + (0.5 * v) * (1.0 - t * t) * (root * (1.0 + (3.0 * 0.044715) * square))
+    return v * half, slope
+
+
+def wide(keep):
+    k = keep.astype(F32)
+    return jnp.concatenate([k, k, k], axis=-1)
+
+
+def fused_kernel(
+    x_ref, w_ref, b_ref, keep_ref, cot_ref,
+    out_ref, sum_ref,
+    edge0, act1, prev1, act2, turned2, turned_cot, turned_keep, act3, pre,
+    slope, through, grad, up_turned, up_out, up2, next1, edge_back,
+    acc, stage_send, stage_recv,
+    send_sem, recv_sem, local_sem, sum_send_sem, sum_recv_sem,
+):
+    windows, frames, ch = x_ref.shape
+    rows = windows * frames
+    y = lax.axis_index("tlo")
+    thi = lax.axis_index("thi")
+    block = thi * 2 + y
+    z = thi // 4
+    cx = lax.rem(thi, 4)
+    xx = cx // 2
+    core = lax.rem(thi, 2)
+
+    def at_block(offset):
+        other = lax.rem(block + offset + 32, 32)
+        return (lax.rem(other, 2), other // 2)
+
+    def at_z(other):
+        return (y, other * 4 + cx)
+
+    partner = {
+        "core": (y, z * 4 + xx * 2 + (1 - core)),
+        "x": (y, z * 4 + (1 - xx) * 2 + core),
+        "y": (1 - y, thi),
+        "z1": at_z(z + 1 - 2 * lax.rem(z, 2)),
+        "z2": at_z(lax.rem(z + 2, 4)),
+    }
+    bit = {"core": core, "x": xx, "y": y, "z1": lax.rem(z, 2), "z2": z // 2}
+
+    barrier = pltpu.get_barrier_semaphore()
+    greeted = [at_block(o) for o in (1, -1, 2, -2)]
+    greeted += [at_z(lax.rem(z + o, 4)) for o in (1, 2, 3)]
+    greeted += [partner["core"], partner["x"], partner["y"]]
+    for device in greeted:
+        pl.semaphore_signal(barrier, inc=1, device_id=device, device_id_type=MESH)
+
+    pending = []
+
+    def send(src, dst, index, device):
+        copy = pltpu.make_async_remote_copy(
+            src_ref=src, dst_ref=dst, send_sem=send_sem.at[index], recv_sem=recv_sem.at[index],
+            device_id=device, device_id_type=MESH,
+        )
+        copy.start()
+        pending.append(copy)
+        return copy
+
+    half = frames // 2
+    quarter = frames // 4
+    pl.semaphore_wait(barrier, len(greeted))
+
+    edge_copy = send(x_ref.at[:, half:, :], edge0.at[:, :half, :], 0, at_block(1))
+
+    def turn(src, dst, first, local):
+        own = pltpu.make_async_copy(src.at[z], dst.at[z], local_sem.at[local])
+        own.start()
+        copies = []
+        for o in (1, 2, 3):
+            other = lax.rem(z + o, 4)
+            copies.append(send(src.at[other], dst.at[z], first + o - 1, at_z(other)))
+        return own, copies
+
+    def arrive(turned):
+        own, copies = turned
+        own.wait()
+        for copy in copies:
+            copy.wait_recv()
+
+    edge0[:, half:, :] = x_ref[...]
+    bias = b_ref[...]
+
+    def forward(level, current, keep, nxt):
+        def body(i, _):
+            pair = pl.ds(2 * i, 2)
+            gelu, d = gelu_and_slope(pre[pair].reshape(2 * frames, ch))
+            slope[level, pair] = d.reshape(2, frames, ch)
+            if nxt is not None:
+                total = current[pair].astype(F32) + gelu.reshape(2, frames, ch)
+                nxt[pair] = (wide(keep[pair]) * total).astype(BF16)
+            return 0
+        lax.fori_loop(0, 2, body, 0)
+
+    def add_tap(level, tap, load, first=False):
+        def body(i, _):
+            pair = pl.ds(2 * i, 2)
+            term = rows_times(load(pair).reshape(2 * frames, ch), w_ref[level, tap])
+            if first:
+                term = term + bias[level : level + 1]
+                pre[pair] = term.reshape(2, frames, ch)
+            else:
+                pre[pair] = pre[pair] + term.reshape(2, frames, ch)
+            return 0
+        lax.fori_loop(0, 2, body, 0)
+
+    add_tap(0, 0, lambda p: x_ref[p], True)
+    edge_copy.wait_recv()
+
+    @pl.when(block == 0)
+    def _():
+        edge0[:, :half, :] = jnp.zeros((windows, half, ch), BF16)
+
+    add_tap(0, 1, lambda p: edge0[p, quarter : quarter + frames])
+    add_tap(0, 2, lambda p: edge0[p, 0:frames])
+    forward(0, x_ref, keep_ref, act1)
+
+    one = send(act1, prev1.at[0], 1, at_block(1))
+    two = send(act1, prev1.at[1], 2, at_block(2))
+    cot_turn = turn(cot_ref, turned_cot, 3, 0)
+    keep_turn = turn(keep_ref, turned_keep, 6, 1)
+    add_tap(1, 0, lambda p: act1[p], True)
+    two.wait_recv()
+
+    @pl.when(block < 2)
+    def _():
+        prev1[1] = jnp.zeros((windows, frames, ch), BF16)
+
+    add_tap(1, 2, lambda p: prev1[1, p])
+    one.wait_recv()
+
+    @pl.when(block < 1)
+    def _():
+        prev1[0] = jnp.zeros((windows, frames, ch), BF16)
+
+    add_tap(1, 1, lambda p: prev1[0, p])
+    forward(1, act1, keep_ref, act2)
+
+    act_turn = turn(act2, turned2, 9, 2)
+    acc[10 * ch :, :] = jnp.zeros((UNITS * UNIT_ROWS - 10 * ch, ch), F32)
+    arrive(keep_turn)
+    arrive(cot_turn)
+    arrive(act_turn)
+    add_tap(2, 0, lambda p: turned2[p], True)
+    pre[1:4] += rows_times(turned2[0:3].reshape(3 * frames, ch), w_ref[2, 1]).reshape(3, frames, ch)
+    pre[2:4] += rows_times(turned2[0:2].reshape(2 * frames, ch), w_ref[2, 2]).reshape(2, frames, ch)
+    forward(2, turned2, turned_keep, act3)
+    add_tap(3, 0, lambda p: act3[p], True)
+    forward(3, None, None, None)
+
+    def pull_back(level, upstream, keep):
+        def body(i, total):
+            pair = pl.ds(2 * i, 2)
+            t = wide(keep[pair]) * upstream[pair].astype(F32)
+            through[pair] = t
+            g = (t * slope[level, pair]).astype(BF16)
+            grad[level, pair] = g
+            return total + jnp.sum(g.astype(F32).reshape(2 * frames, ch), axis=0, keepdims=True)
+        total = lax.fori_loop(0, 2, body, jnp.zeros((1, ch), F32))
+        acc[10 * ch + 8 * level : 10 * ch + 8 * level + 1, :] = total
+
+    def back_tap(level, tap, load):
+        def body(i, _):
+            pair = pl.ds(2 * i, 2)
+            term = rows_times_t(load(pair).reshape(2 * frames, ch), w_ref[level, tap])
+            through[pair] = through[pair] + term.reshape(2, frames, ch)
+            return 0
+        lax.fori_loop(0, 2, body, 0)
+
+    def put_weight(slot, a, g):
+        acc[slot * ch : (slot + 1) * ch, :] = t_times_rows(a, g)
+
+    pull_back(3, turned_cot, turned_keep)
+    back_tap(3, 0, lambda p: grad[3, p])
+    up_turned[...] = through[...].astype(BF16)
+    pull_back(2, up_turned, turned_keep)
+    back_tap(2, 0, lambda p: grad[2, p])
+    through[0:3] += rows_times_t(grad[2, 1:4].reshape(3 * frames, ch), w_ref[2, 1]).reshape(3, frames, ch)
+    through[0:2] += rows_times_t(grad[2, 2:4].reshape(2 * frames, ch), w_ref[2, 2]).reshape(2, frames, ch)
+    up_out[...] = through[...].astype(BF16)
+    up_turn = turn(up_out, up2, 12, 3)
+    put_weight(0, act3[...].reshape(rows, ch), grad[3].reshape(rows, ch))
+    for tap in range(3):
+        n = 4 - tap
+        put_weight(1 + tap, turned2[0:n].reshape(n * frames, ch), grad[2, tap:4].reshape(n * frames, ch))
+
+    orders = (("x", "y", "z1", "z2"), ("y", "x", "z1", "z2"))
+
+    def plan(unit):
+        base = unit * UNIT_ROWS
+        size = UNIT_ROWS // 2
+        steps = [[("core", base + (1 - core) * size, base + core * size, size, base)]]
+        for _ in range(4):
+            steps.append([])
+        landing = base + size
+        for h, order in enumerate(orders):
+            at = base + core * size + h * (size // 2)
+            n = size // 2
+            for s, name in enumerate(order):
+                n = n // 2
+                steps[s + 1].append((name, at + (1 - bit[name]) * n, at + bit[name] * n, n, landing))
+                at = at + bit[name] * n
+                landing += n
+        return steps
+
+    plans = [plan(u) for u in range(UNITS)]
+    flying = {}
+
+    def aligned(at, n):
+        return pl.ds(at if isinstance(at, int) else pl.multiple_of(at, 16), n)
+
+    def sum_copy(src, dst, unit, index, name):
+        copy = pltpu.make_async_remote_copy(
+            src_ref=src, dst_ref=dst, send_sem=sum_send_sem.at[unit, index],
+            recv_sem=sum_recv_sem.at[unit, index], device_id=partner[name], device_id_type=MESH,
+        )
+        copy.start()
+        pending.append(copy)
+        return copy
+
+    def begin(unit, stage):
+        copies = []
+        if stage < 5:
+            for h, (name, give, _, n, landing) in enumerate(plans[unit][stage]):
+                stage_send[aligned(give, n), :] = acc[aligned(give, n), :].astype(BF16)
+                copies.append(sum_copy(
+                    stage_send.at[aligned(give, n), :], stage_recv.at[pl.ds(landing, n), :],
+                    unit, 2 * stage + h, name))
+        else:
+            for h, (name, _, own, n, _) in enumerate(plans[unit][9 - stage]):
+                span = aligned(own, n)
+                if stage == 5:
+                    sum_ref[span, :] = acc[span, :].astype(BF16)
+                copies.append(sum_copy(sum_ref.at[span, :], sum_ref.at[span, :], unit, 2 * stage + h, name))
+        flying[unit, stage] = copies
+
+    def finish(unit, stage):
+        for copy in flying[unit, stage]:
+            copy.wait_recv()
+        if stage < 5:
+            for _, _, own, n, landing in plans[unit][stage]:
+                span = aligned(own, n)
+                acc[span, :] = acc[span, :] + stage_recv[landing : landing + n, :].astype(F32)
+
+    def advance(unit, stage):
+        if stage > 0:
+            finish(unit, stage - 1)
+        if stage < 10:
+            begin(unit, stage)
+
+    advance(0, 0)
+    arrive(up_turn)
+    pull_back(1, up2, keep_ref)
+    back_one = send(grad.at[1], next1.at[0], 15, at_block(-1))
+    back_two = send(grad.at[1], next1.at[1], 16, at_block(-2))
+    advance(0, 1)
+    g1 = grad[1].reshape(rows, ch)
+    put_weight(4, act1[...].reshape(rows, ch), g1)
+    put_weight(5, prev1[0].reshape(rows, ch), g1)
+    advance(0, 2)
+    advance(1, 0)
+    put_weight(6, prev1[1].reshape(rows, ch), g1)
+    back_tap(1, 0, lambda p: grad[1, p])
+    advance(1, 1)
+    back_two.wait_recv()
+
+    @pl.when(block >= 30)
+    def _():
+        next1[1] = jnp.zeros((windows, frames, ch), BF16)
+
+    back_tap(1, 2, lambda p: next1[1, p])
+    back_one.wait_recv()
+
+    @pl.when(block >= 31)
+    def _():
+        next1[0] = jnp.zeros((windows, frames, ch), BF16)
+
+    back_tap(1, 1, lambda p: next1[0, p])
+    up_turned[...] = through[...].astype(BF16)
+    pull_back(0, up_turned, keep_ref)
+    edge_back[:, :frames, :] = grad[0]
+    back_edge = send(grad.at[0, :, :half, :], edge_back.at[:, frames:, :], 17, at_block(-1))
+    advance(0, 3)
+    g0 = grad[0].reshape(rows, ch)
+    put_weight(7, x_ref[...].reshape(rows, ch), g0)
+    advance(2, 0)
+    put_weight(8, edge0[:, quarter : quarter + frames].reshape(rows, ch), g0)
+    put_weight(9, edge0[:, 0:frames].reshape(rows, ch), g0)
+    advance(3, 0)
+    advance(1, 2)
+    advance(2, 1)
+    back_tap(0, 0, lambda p: grad[0, p])
+    advance(3, 1)
+    back_edge.wait_recv()
+
+    @pl.when(block >= 31)
+    def _():
+        edge_back[:, frames:, :] = jnp.zeros((windows, half, ch), BF16)
+
+    back_tap(0, 1, lambda p: edge_back[p, quarter : quarter + frames])
+    back_tap(0, 2, lambda p: edge_back[p, half : half + frames])
+    out_ref[...] = through[...].astype(BF16)
+    at = [3, 2, 1, 1]
+    while min(at) < 10:
+        for u in range(UNITS):
+            if at[u] < 10:
+                at[u] += 1
+                advance(u, at[u])
+    for copy in pending:
+        copy.wait_send()
+
+
+def fused_shards(frames_in, weights, biases, valid_mask, cotangent):
+    windows, frames, ch = frames_in.shape
+    levels = weights.shape[0]
+    keep = jnp.broadcast_to(valid_mask.astype(BF16)[:, :, None], (windows, frames, ch // 3))
+    vmem = pl.BlockSpec(memory_space=pltpu.VMEM)
+    block = (windows, frames, ch)
+    sum_rows = UNITS * UNIT_ROWS
+    grad_in, sums = pl.pallas_call(
+        fused_kernel,
+        out_shape=(
+            jax.ShapeDtypeStruct(block, BF16),
+            jax.ShapeDtypeStruct((sum_rows, ch), BF16),
+        ),
+        in_specs=[vmem] * 5,
+        out_specs=(vmem, vmem),
+        scratch_shapes=[
+            pltpu.VMEM((windows, frames + frames // 2, ch), BF16),
+            pltpu.VMEM(block, BF16),
+            pltpu.VMEM((2,) + block, BF16),
+            pltpu.VMEM(block, BF16),
+            pltpu.VMEM(block, BF16),
+            pltpu.VMEM(block, BF16),
+            pltpu.VMEM((windows, frames, ch // 3), BF16),
+            pltpu.VMEM(block, BF16),
+            pltpu.VMEM(block, F32),
+            pltpu.VMEM((levels,) + block, F32),
+            pltpu.VMEM(block, F32),
+            pltpu.VMEM((levels,) + block, BF16),
+            pltpu.VMEM(block, BF16),
+            pltpu.VMEM(block, BF16),
+            pltpu.VMEM(block, BF16),
+            pltpu.VMEM((2,) + block, BF16),
+            pltpu.VMEM((windows, frames + frames // 2, ch), BF16),
+            pltpu.VMEM((sum_rows, ch), F32),
+            pltpu.VMEM((sum_rows, ch), BF16),
+            pltpu.VMEM((sum_rows, ch), BF16),
+            pltpu.SemaphoreType.DMA((18,)),
+            pltpu.SemaphoreType.DMA((18,)),
+            pltpu.SemaphoreType.DMA((4,)),
+            pltpu.SemaphoreType.DMA((UNITS, 20)),
+            pltpu.SemaphoreType.DMA((UNITS, 20)),
+        ],
+        compiler_params=pltpu.CompilerParams(
+            collective_id=0, has_side_effects=True, vmem_limit_bytes=48 * 1024 * 1024
+        ),
+    )(frames_in, weights, biases, keep, cotangent)
+    factor = 1.0 / math.sqrt(windows * frames * lax.axis_size("tlo") * lax.axis_size("thi"))
+    scaled = sums.astype(F32) * factor
+    grads = scaled[: 10 * ch].reshape(10, ch, ch)
+    none = jnp.zeros((2, ch, ch), F32)
+    weight_grad = jnp.concatenate([grads[7:10], grads[4:7], grads[1:4], grads[0:1], none])
+    bias_grad = scaled[10 * ch : 10 * ch + 8 * levels].reshape(levels, 8, ch)[:, 0]
+    return (grad_in, weight_grad.reshape(levels, 3, ch, ch), bias_grad)
 
 
 def shifted(block, axis, distance):
@@ -117,8 +511,9 @@
 
 
 def solution(mesh):
+    fused = mesh.shape["tlo"] == 2 and mesh.shape["thi"] == 16
     return jax.shard_map(
-        shards,
+        fused_shards if fused else shards,
         mesh=mesh,
         in_specs=(
             P(None, ("thi", "tlo"), None),

time: 337 us -> 124 us (0.37)
  waiting for transfers between devices: 177 us -> 0 us
  Pallas kernels: 0 us -> 115 us
  blocking collectives: 46.6 us -> 0 us
  starting transfers between devices: 37.9 us -> 0 us
  matrix products: 23.3 us -> 0 us
  other arithmetic: 16.7 us -> 1.09 us
  between operations: 14.6 us -> 0.74 us
  local copies, waits for them, and re-layouts: 19.2 us -> 6.68 us
    pallas_call x0 -> x1, Pallas kernels: none -> 115 us  [fused_shards(): pl.pallas_call(fused_kernel, out_shape=(jax.ShapeDtypeStruct(block, BF16)...]
    psum x1 -> x0, waiting for transfers between devices: 105 us -> none  [reduce_grads(): return lax.psum((weight_part, bias_part), ('tlo', 'thi'))]
    ppermute x14 -> x0, waiting for transfers between devices: 71.6 us -> none  [the longest x10 55.4 us: from_behind(): lax.ppermute(value, axis, [(source, source + steps) for source in range(f...]
    psum x1 -> x0, blocking collectives: 46.6 us -> none  [reduce_grads(): return lax.psum((weight_part, bias_part), ('tlo', 'thi'))]
    ppermute x14 -> x0, starting transfers between devices: 37.9 us -> none  [the longest x10 31.9 us: from_behind(): lax.ppermute(value, axis, [(source, source + steps) for source in range(f...]
    dot_general x12 -> x0, matrix products: 23.3 us -> none  [the longest x4 12.2 us: shards(): jnp.dot(gathered, mirrored, preferred_element_type=jnp.float32)]
    transpose x5 -> x0, local copies, waits for them, and re-layouts: 13.9 us -> none  [shards(): jnp.transpose(weights[level], (0, 2, 1)).reshape(widths, channels)]
    mul x2 -> x1, other arithmetic: 7.02 us -> 0.41 us  [fused_shards(): scaled = sums.astype(F32) * factor]
  transfers between devices with their start and end apart: 15 -> 0, of which waited for: 10 -> 0; matrix products, arithmetic and copies ran while one was open for 7% -> 0% of each run, Pallas kernels for 0% -> 0%
where the time goes in v1:
time: 124 us; the launch traced here: 123 us
  Pallas kernels  115 us (93%)
  local copies, waits for them, and re-layouts  6.68 us (5%)
    pallas_call x1, Pallas kernels, fused_shards(): pl.pallas_call(fused_kernel, out_shape=(jax.ShapeDtypeStruct(block, BF16)...  115 us
    unnamed x14, local copies, waits for them, and re-layouts  6.12 us

profile of v1, /device:TPU:1, one launch (start us, length us, event | category | flops | bytes accessed | tf_op | source)
XLA Modules:
  0.0 123.2 jit_solution(3784617426794276996)
XLA Ops:
  0.6 0.7 convert_element_type.6
  1.3 0.1 broadcast_in_dim.4.keep_ref
  1.5 0.0 copy-start
  1.5 1.0 copy-done
  2.5 0.0 copy-start.1
  2.5 1.0 copy-done.1
  3.5 0.0 copy-start.2
  3.5 0.7 copy-done.2
  4.1 114.7 %shard_map.76 = (bf16[4,128,384]{2,1,0:T(8,128)(2,1)S(1)}, bf16[4096,384]{1,0:T(8,128)(2,1)S(1)}) custom-call(bf16[4,128,384]{2,1,0:T(8,128)(2,1)S(1)} %copy-done, bf16[4,3,384,384]{3,2,1,0:T(8,128)(2,1)} %w_ref.1, f32[4,384]{1,0:T(4,128)S(1)} %copy-done.2, bf16[4,128,128]{2,1,0:T(8,128)(2,1)S(1)} %broadcast_in_dim.4.keep_ref, bf16[4,128,384]{2,1,0:T(8,128)(2,1)S(1)} %copy-done.1), custom_call_target="tpu_custom_call" | custom-call | tf_op jit(solution)/shard_map/pallas_call | solution.py:355
  118.9 0.4 convert_multiply_fusion
  119.3 0.3 fusion.1
  119.6 0.1 constant_dynamic-update-slice_fusion.2
  119.8 0.1 constant_dynamic-update-slice_fusion.1
  119.9 0.1 constant_dynamic-update-slice_fusion
  120.1 0.1 broadcast_dynamic-update-slice_fusion
  120.1 0.0 copy-start.3
  120.2 0.7 copy.11
  120.8 1.3 %copy.17 = bf16[4,128,384]{2,1,0:T(8,128)(2,1)} copy(bf16[4,128,384]{2,1,0:T(8,128)(2,1)S(1)} %get-tuple-element.13) | data formatting | bytes 786432
  122.1 1.1 copy-done.3
  (3 shorter events, 0.1 us)
Async XLA Ops:
  1.5 1.0 copy-start
  2.5 1.0 copy-start.1
  3.5 0.7 copy-start.2
  120.1 3.1 %copy-start.3 = (f32[12,384,384]{2,1,0:T(8,128)}, f32[12,384,384]{2,1,0:T(8,128)S(1)}, u32[]{:S(2)}) copy-start(f32[12,384,384]{2,1,0:T(8,128)S(1)} %broadcast_dynamic-update-slice_fusion) | copy-start | bytes 21233668

commit v2 on v1

--- a/solution.py
+++ b/solution.py
@@ -35,18 +35,13 @@
     return v * half, slope
 
 
-def wide(keep):
-    k = keep.astype(F32)
-    return jnp.concatenate([k, k, k], axis=-1)
-
-
 def fused_kernel(
     x_ref, w_ref, b_ref, keep_ref, cot_ref,
     out_ref, sum_ref,
-    edge0, act1, prev1, act2, turned2, turned_cot, turned_keep, act3, pre,
-    slope, through, grad, up_turned, up_out, up2, next1, edge_back,
+    edge0, act1, prev1, act2, turned2, turned_cot, turned_keep, act3, own_wide, turned_wide,
+    slope, through, grad, grad2, up_out, up2, next1, edge_back,
     acc, stage_send, stage_recv,
-    send_sem, recv_sem, local_sem, sum_send_sem, sum_recv_sem,
+    send_sem, recv_sem, sum_send_sem, sum_recv_sem,
 ):
     windows, frames, ch = x_ref.shape
     rows = windows * frames
@@ -58,6 +53,10 @@
     xx = cx // 2
     core = lax.rem(thi, 2)
 
+    near_z = z + 1 - 2 * lax.rem(z, 2)
+    far_z = lax.rem(z + 2, 4)
+    others = (far_z, 3 - z, near_z)
+
     def at_block(offset):
         other = lax.rem(block + offset + 32, 32)
         return (lax.rem(other, 2), other // 2)
@@ -69,14 +68,14 @@
         "core": (y, z * 4 + xx * 2 + (1 - core)),
         "x": (y, z * 4 + (1 - xx) * 2 + core),
         "y": (1 - y, thi),
-        "z1": at_z(z + 1 - 2 * lax.rem(z, 2)),
-        "z2": at_z(lax.rem(z + 2, 4)),
+        "z1": at_z(near_z),
+        "z2": at_z(far_z),
     }
     bit = {"core": core, "x": xx, "y": y, "z1": lax.rem(z, 2), "z2": z // 2}
 
     barrier = pltpu.get_barrier_semaphore()
     greeted = [at_block(o) for o in (1, -1, 2, -2)]
-    greeted += [at_z(lax.rem(z + o, 4)) for o in (1, 2, 3)]
+    greeted += [at_z(other) for other in others]
     greeted += [partner["core"], partner["x"], partner["y"]]
     for device in greeted:
         pl.semaphore_signal(barrier, inc=1, device_id=device, device_id_type=MESH)
@@ -96,128 +95,136 @@
     quarter = frames // 4
     pl.semaphore_wait(barrier, len(greeted))
 
-    edge_copy = send(x_ref.at[:, half:, :], edge0.at[:, :half, :], 0, at_block(1))
-
-    def turn(src, dst, first, local):
-        own = pltpu.make_async_copy(src.at[z], dst.at[z], local_sem.at[local])
-        own.start()
-        copies = []
-        for o in (1, 2, 3):
-            other = lax.rem(z + o, 4)
-            copies.append(send(src.at[other], dst.at[z], first + o - 1, at_z(other)))
-        return own, copies
-
-    def arrive(turned):
-        own, copies = turned
-        own.wait()
-        for copy in copies:
-            copy.wait_recv()
-
+    order = others + (z,)
+    edge_copies = [
+        send(x_ref.at[w, half:, :], edge0.at[w, :half, :], w, at_block(1)) for w in order
+    ]
+    keep_copies = [
+        send(keep_ref.at[o], turned_keep.at[z], 40 + i, at_z(o)) for i, o in enumerate(others)
+    ]
+    cot_copies = [
+        send(cot_ref.at[o], turned_cot.at[z], 43 + i, at_z(o)) for i, o in enumerate(others)
+    ]
+    turned_keep[z] = keep_ref[z]
+    turned_cot[z] = cot_ref[z]
+    zeros = jnp.zeros((frames, ch), BF16)
+    turned2[0] = zeros
+    turned2[1] = zeros
+    grad2[4] = zeros
+    grad2[5] = zeros
+    acc[10 * ch :, :] = jnp.zeros((UNITS * UNIT_ROWS - 10 * ch, ch), F32)
     edge0[:, half:, :] = x_ref[...]
     bias = b_ref[...]
-
-    def forward(level, current, keep, nxt):
-        def body(i, _):
-            pair = pl.ds(2 * i, 2)
-            gelu, d = gelu_and_slope(pre[pair].reshape(2 * frames, ch))
-            slope[level, pair] = d.reshape(2, frames, ch)
-            if nxt is not None:
-                total = current[pair].astype(F32) + gelu.reshape(2, frames, ch)
-                nxt[pair] = (wide(keep[pair]) * total).astype(BF16)
-            return 0
-        lax.fori_loop(0, 2, body, 0)
-
-    def add_tap(level, tap, load, first=False):
-        def body(i, _):
-            pair = pl.ds(2 * i, 2)
-            term = rows_times(load(pair).reshape(2 * frames, ch), w_ref[level, tap])
-            if first:
-                term = term + bias[level : level + 1]
-                pre[pair] = term.reshape(2, frames, ch)
-            else:
-                pre[pair] = pre[pair] + term.reshape(2, frames, ch)
-            return 0
-        lax.fori_loop(0, 2, body, 0)
-
-    add_tap(0, 0, lambda p: x_ref[p], True)
-    edge_copy.wait_recv()
-
-    @pl.when(block == 0)
-    def _():
-        edge0[:, :half, :] = jnp.zeros((windows, half, ch), BF16)
-
-    add_tap(0, 1, lambda p: edge0[p, quarter : quarter + frames])
-    add_tap(0, 2, lambda p: edge0[p, 0:frames])
-    forward(0, x_ref, keep_ref, act1)
-
-    one = send(act1, prev1.at[0], 1, at_block(1))
-    two = send(act1, prev1.at[1], 2, at_block(2))
-    cot_turn = turn(cot_ref, turned_cot, 3, 0)
-    keep_turn = turn(keep_ref, turned_keep, 6, 1)
-    add_tap(1, 0, lambda p: act1[p], True)
-    two.wait_recv()
-
-    @pl.when(block < 2)
-    def _():
-        prev1[1] = jnp.zeros((windows, frames, ch), BF16)
-
-    add_tap(1, 2, lambda p: prev1[1, p])
-    one.wait_recv()
-
-    @pl.when(block < 1)
-    def _():
-        prev1[0] = jnp.zeros((windows, frames, ch), BF16)
-
-    add_tap(1, 1, lambda p: prev1[0, p])
-    forward(1, act1, keep_ref, act2)
-
-    act_turn = turn(act2, turned2, 9, 2)
-    acc[10 * ch :, :] = jnp.zeros((UNITS * UNIT_ROWS - 10 * ch, ch), F32)
-    arrive(keep_turn)
-    arrive(cot_turn)
-    arrive(act_turn)
-    add_tap(2, 0, lambda p: turned2[p], True)
-    pre[1:4] += rows_times(turned2[0:3].reshape(3 * frames, ch), w_ref[2, 1]).reshape(3, frames, ch)
-    pre[2:4] += rows_times(turned2[0:2].reshape(2 * frames, ch), w_ref[2, 2]).reshape(2, frames, ch)
-    forward(2, turned2, turned_keep, act3)
-    add_tap(3, 0, lambda p: act3[p], True)
-    forward(3, None, None, None)
-
-    def pull_back(level, upstream, keep):
-        def body(i, total):
-            pair = pl.ds(2 * i, 2)
-            t = wide(keep[pair]) * upstream[pair].astype(F32)
-            through[pair] = t
-            g = (t * slope[level, pair]).astype(BF16)
-            grad[level, pair] = g
-            return total + jnp.sum(g.astype(F32).reshape(2 * frames, ch), axis=0, keepdims=True)
-        total = lax.fori_loop(0, 2, body, jnp.zeros((1, ch), F32))
-        acc[10 * ch + 8 * level : 10 * ch + 8 * level + 1, :] = total
-
-    def back_tap(level, tap, load):
-        def body(i, _):
-            pair = pl.ds(2 * i, 2)
-            term = rows_times_t(load(pair).reshape(2 * frames, ch), w_ref[level, tap])
-            through[pair] = through[pair] + term.reshape(2, frames, ch)
-            return 0
-        lax.fori_loop(0, 2, body, 0)
+    across = lax.broadcasted_iota(jnp.int32, (frames, frames), 0) == lax.broadcasted_iota(
+        jnp.int32, (frames, frames), 1
+    )
+    ones = jnp.ones((frames, ch), BF16)
+
+    def widen(row):
+        diagonal = jnp.where(across, jnp.broadcast_to(row, (frames, frames)), 0.0)
+        return rows_times(diagonal.astype(BF16), ones)
+
+    for w in range(windows):
+        own_wide[w] = widen(keep_ref[w, 0:1, :])
+
+    def taps(level, a, b, c):
+        total = rows_times(a, w_ref[level, 0]) + rows_times(b, w_ref[level, 1])
+        return total + rows_times(c, w_ref[level, 2])
+
+    def taps_back(level, a, b, c):
+        total = rows_times_t(a, w_ref[level, 0]) + rows_times_t(b, w_ref[level, 1])
+        return total + rows_times_t(c, w_ref[level, 2])
+
+    one_copies, two_copies = [], []
+    for w, copy in zip(order, edge_copies):
+        copy.wait_recv()
+
+        @pl.when(block == 0)
+        def _():
+            edge0[w, :half, :] = jnp.zeros((half, ch), BF16)
+
+        now = x_ref[w]
+        total = taps(0, now, edge0[w, quarter : quarter + frames], edge0[w, 0:frames])
+        gelu, d = gelu_and_slope(total + bias[0:1])
+        slope[0, w] = d
+        act1[w] = (own_wide[w] * (now.astype(F32) + gelu)).astype(BF16)
+        one_copies.append(send(act1.at[w], prev1.at[0, w], 4 + w, at_block(1)))
+        two_copies.append(send(act1.at[w], prev1.at[1, w], 8 + w, at_block(2)))
+
+    act_copies = []
+    for i, w in enumerate(order):
+        one_copies[i].wait_recv()
+        two_copies[i].wait_recv()
+
+        @pl.when(block < 1)
+        def _():
+            prev1[0, w] = zeros
+
+        @pl.when(block < 2)
+        def _():
+            prev1[1, w] = zeros
+
+        now = act1[w]
+        total = taps(1, now, prev1[0, w], prev1[1, w])
+        gelu, d = gelu_and_slope(total + bias[1:2])
+        slope[1, w] = d
+        result = (own_wide[w] * (now.astype(F32) + gelu)).astype(BF16)
+        if i < 3:
+            act2[w] = result
+            act_copies.append(send(act2.at[w], turned2.at[2 + z], 46 + i, at_z(w)))
+        else:
+            turned2[2 + z] = result
+
+    for copy in keep_copies:
+        copy.wait_recv()
+    for w in range(windows):
+        turned_wide[w] = widen(turned_keep[w, 0:1, :])
+    for copy in cot_copies + act_copies:
+        copy.wait_recv()
+
+    def flat(ref, first):
+        return ref[pl.ds(first, 2)].reshape(2 * frames, ch)
+
+    def put(ref, first, value):
+        ref[pl.ds(first, 2)] = value.reshape(2, frames, ch)
+
+    def add_bias(level, g):
+        at = 10 * ch + 8 * level
+        acc[at : at + 1, :] += jnp.sum(g.astype(F32), axis=0, keepdims=True)
+
+    def far_levels(i, _):
+        first = 2 * i
+        now = flat(turned2, 2 + first)
+        keep = flat(turned_wide, first)
+        total = taps(2, now, flat(turned2, 1 + first), flat(turned2, first))
+        gelu, d = gelu_and_slope(total + bias[2:3])
+        last = (keep * (now.astype(F32) + gelu)).astype(BF16)
+        put(act3, first, last)
+        _, d3 = gelu_and_slope(rows_times(last, w_ref[3, 0]) + bias[3:4])
+        t = keep * flat(turned_cot, first).astype(F32)
+        g = (t * d3).astype(BF16)
+        grad[0, pl.ds(first, 2)] = g.reshape(2, frames, ch)
+        add_bias(3, g)
+        t = keep * (t + rows_times_t(g, w_ref[3, 0])).astype(BF16).astype(F32)
+        g = (t * d).astype(BF16)
+        put(grad2, first, g)
+        put(through, first, t)
+        add_bias(2, g)
+        return 0
+
+    lax.fori_loop(0, 2, far_levels, 0)
+
+    up_copies = []
+    for i, w in enumerate(order):
+        result = through[w] + taps_back(2, grad2[w], grad2[w + 1], grad2[w + 2])
+        if i < 3:
+            up_out[w] = result.astype(BF16)
+            up_copies.append(send(up_out.at[w], up2.at[z], 49 + i, at_z(w)))
+        else:
+            up2[z] = result.astype(BF16)
 
     def put_weight(slot, a, g):
         acc[slot * ch : (slot + 1) * ch, :] = t_times_rows(a, g)
-
-    pull_back(3, turned_cot, turned_keep)
-    back_tap(3, 0, lambda p: grad[3, p])
-    up_turned[...] = through[...].astype(BF16)
-    pull_back(2, up_turned, turned_keep)
-    back_tap(2, 0, lambda p: grad[2, p])
-    through[0:3] += rows_times_t(grad[2, 1:4].reshape(3 * frames, ch), w_ref[2, 1]).reshape(3, frames, ch)
-    through[0:2] += rows_times_t(grad[2, 2:4].reshape(2 * frames, ch), w_ref[2, 2]).reshape(2, frames, ch)
-    up_out[...] = through[...].astype(BF16)
-    up_turn = turn(up_out, up2, 12, 3)
-    put_weight(0, act3[...].reshape(rows, ch), grad[3].reshape(rows, ch))
-    for tap in range(3):
-        n = 4 - tap
-        put_weight(1 + tap, turned2[0:n].reshape(n * frames, ch), grad[2, tap:4].reshape(n * frames, ch))
 
     orders = (("x", "y", "z1", "z2"), ("y", "x", "z1", "z2"))
 
@@ -283,58 +290,82 @@
         if stage < 10:
             begin(unit, stage)
 
+    back_order = (z, near_z, far_z, 3 - z)
+    arrivals = (None, up_copies[2], up_copies[0], up_copies[1])
+    back_one, back_two = [], []
+
+    def start_one(i):
+        w = back_order[i]
+        if i > 0:
+            arrivals[i].wait_recv()
+        t = own_wide[w] * up2[w].astype(F32)
+        g = (t * slope[1, w]).astype(BF16)
+        through[w] = t
+        grad[1, w] = g
+        back_one.append(send(grad.at[1, w], next1.at[0, w], 12 + w, at_block(-1)))
+        back_two.append(send(grad.at[1, w], next1.at[1, w], 16 + w, at_block(-2)))
+        add_bias(1, g)
+
+    start_one(0)
+    put_weight(0, act3[...].reshape(rows, ch), grad[0].reshape(rows, ch))
+    for tap in range(3):
+        n = 4 - tap
+        put_weight(1 + tap, turned2[2 : 2 + n].reshape(n * frames, ch), grad2[tap:4].reshape(n * frames, ch))
+    for i in range(1, 4):
+        start_one(i)
     advance(0, 0)
-    arrive(up_turn)
-    pull_back(1, up2, keep_ref)
-    back_one = send(grad.at[1], next1.at[0], 15, at_block(-1))
-    back_two = send(grad.at[1], next1.at[1], 16, at_block(-2))
-    advance(0, 1)
     g1 = grad[1].reshape(rows, ch)
     put_weight(4, act1[...].reshape(rows, ch), g1)
     put_weight(5, prev1[0].reshape(rows, ch), g1)
+    put_weight(6, prev1[1].reshape(rows, ch), g1)
+    advance(0, 1)
+    advance(1, 0)
+    back_edges = []
+    for i, w in enumerate(back_order):
+        back_one[i].wait_recv()
+        back_two[i].wait_recv()
+
+        @pl.when(block >= 31)
+        def _():
+            next1[0, w] = zeros
+
+        @pl.when(block >= 30)
+        def _():
+            next1[1, w] = zeros
+
+        total = through[w] + taps_back(1, grad[1, w], next1[0, w], next1[1, w])
+        t = own_wide[w] * total.astype(BF16).astype(F32)
+        g = (t * slope[0, w]).astype(BF16)
+        through[w] = t
+        grad[2, w] = g
+        edge_back[w, :frames, :] = g
+        back_edges.append(
+            send(grad.at[2, w, :half, :], edge_back.at[w, frames:, :], 20 + w, at_block(-1))
+        )
+        add_bias(0, g)
     advance(0, 2)
-    advance(1, 0)
-    put_weight(6, prev1[1].reshape(rows, ch), g1)
-    back_tap(1, 0, lambda p: grad[1, p])
     advance(1, 1)
-    back_two.wait_recv()
-
-    @pl.when(block >= 30)
-    def _():
-        next1[1] = jnp.zeros((windows, frames, ch), BF16)
-
-    back_tap(1, 2, lambda p: next1[1, p])
-    back_one.wait_recv()
-
-    @pl.when(block >= 31)
-    def _():
-        next1[0] = jnp.zeros((windows, frames, ch), BF16)
-
-    back_tap(1, 1, lambda p: next1[0, p])
-    up_turned[...] = through[...].astype(BF16)
-    pull_back(0, up_turned, keep_ref)
-    edge_back[:, :frames, :] = grad[0]
-    back_edge = send(grad.at[0, :, :half, :], edge_back.at[:, frames:, :], 17, at_block(-1))
-    advance(0, 3)
-    g0 = grad[0].reshape(rows, ch)
+    g0 = grad[2].reshape(rows, ch)
     put_weight(7, x_ref[...].reshape(rows, ch), g0)
     advance(2, 0)
     put_weight(8, edge0[:, quarter : quarter + frames].reshape(rows, ch), g0)
     put_weight(9, edge0[:, 0:frames].reshape(rows, ch), g0)
     advance(3, 0)
+    advance(0, 3)
     advance(1, 2)
     advance(2, 1)
-    back_tap(0, 0, lambda p: grad[0, p])
     advance(3, 1)
-    back_edge.wait_recv()
-
-    @pl.when(block >= 31)
-    def _():
-        edge_back[:, frames:, :] = jnp.zeros((windows, half, ch), BF16)
-
-    back_tap(0, 1, lambda p: edge_back[p, quarter : quarter + frames])
-    back_tap(0, 2, lambda p: edge_back[p, half : half + frames])
-    out_ref[...] = through[...].astype(BF16)
+    for i, w in enumerate(back_order):
+        back_edges[i].wait_recv()
+
+        @pl.when(block >= 31)
+        def _():
+            edge_back[w, frames:, :] = jnp.zeros((half, ch), BF16)
+
+        total = through[w] + taps_back(
+            0, grad[2, w], edge_back[w, quarter : quarter + frames], edge_back[w, half : half + frames]
+        )
+        out_ref[w] = total.astype(BF16)
     at = [3, 2, 1, 1]
     while min(at) < 10:
         for u in range(UNITS):
@@ -348,7 +379,7 @@
 def fused_shards(frames_in, weights, biases, valid_mask, cotangent):
     windows, frames, ch = frames_in.shape
     levels = weights.shape[0]
-    keep = jnp.broadcast_to(valid_mask.astype(BF16)[:, :, None], (windows, frames, ch // 3))
+    keep = jnp.broadcast_to(valid_mask.astype(F32)[:, None, :], (windows, 8, frames))
     vmem = pl.BlockSpec(memory_space=pltpu.VMEM)
     block = (windows, frames, ch)
     sum_rows = UNITS * UNIT_ROWS
@@ -365,15 +396,16 @@
             pltpu.VMEM(block, BF16),
             pltpu.VMEM((2,) + block, BF16),
             pltpu.VMEM(block, BF16),
+            pltpu.VMEM((windows + 2, frames, ch), BF16),
             pltpu.VMEM(block, BF16),
-            pltpu.VMEM(block, BF16),
-            pltpu.VMEM((windows, frames, ch // 3), BF16),
+            pltpu.VMEM((windows, 8, frames), F32),
             pltpu.VMEM(block, BF16),
             pltpu.VMEM(block, F32),
-            pltpu.VMEM((levels,) + block, F32),
             pltpu.VMEM(block, F32),
-            pltpu.VMEM((levels,) + block, BF16),
-            pltpu.VMEM(block, BF16),
+            pltpu.VMEM((2,) + block, F32),
+            pltpu.VMEM(block, F32),
+            pltpu.VMEM((3,) + block, BF16),
+            pltpu.VMEM((windows + 2, frames, ch), BF16),
             pltpu.VMEM(block, BF16),
             pltpu.VMEM(block, BF16),
             pltpu.VMEM((2,) + block, BF16),
@@ -381,9 +413,8 @@
             pltpu.VMEM((sum_rows, ch), F32),
             pltpu.VMEM((sum_rows, ch), BF16),
             pltpu.VMEM((sum_rows, ch), BF16),
-            pltpu.SemaphoreType.DMA((18,)),
-            pltpu.SemaphoreType.DMA((18,)),
-            pltpu.SemaphoreType.DMA((4,)),
+            pltpu.SemaphoreType.DMA((52,)),
+            pltpu.SemaphoreType.DMA((52,)),
             pltpu.SemaphoreType.DMA((UNITS, 20)),
             pltpu.SemaphoreType.DMA((UNITS, 20)),
         ],

time: 124 us -> 114 us (0.919)
  Pallas kernels: 115 us -> 105 us
    pallas_call x1, Pallas kernels: 115 us -> 105 us  [fused_shards(): pl.pallas_call(fused_kernel, out_shape=(jax.ShapeDtypeStruct(block, BF16)...]
where the time goes in v2:
time: 114 us
  Pallas kernels  105 us (92%)
  local copies, waits for them, and re-layouts  6.56 us (6%)
    pallas_call x1, Pallas kernels, fused_shards(): pl.pallas_call(fused_kernel, out_shape=(jax.ShapeDtypeStruct(block, BF16)...  105 us
    unnamed x14, local copies, waits for them, and re-layouts  6.12 us

profile of v2, /device:TPU:1, one launch (start us, length us, event | category | flops | bytes accessed | tf_op | source)
XLA Modules:
  0.0 113.9 jit_solution(3397025757258114818)
XLA Ops:
  0.6 0.7 convert_element_type.6
  1.3 0.0 copy-start
  1.3 1.0 copy-done
  2.3 0.0 copy-start.1
  2.3 1.0 copy-done.1
  3.3 0.0 copy-start.2
  3.3 0.7 copy-done.2
  4.0 105.5 %shard_map.76 = (bf16[4,128,384]{2,1,0:T(8,128)(2,1)S(1)}, bf16[4096,384]{1,0:T(8,128)(2,1)S(1)}) custom-call(bf16[4,128,384]{2,1,0:T(8,128)(2,1)S(1)} %copy-done, bf16[4,3,384,384]{3,2,1,0:T(8,128)(2,1)} %w_ref.1, f32[4,384]{1,0:T(4,128)S(1)} %copy-done.2, f32[4,8,128]{2,1,0:T(8,128)S(1)} %broadcast_in_dim.4.keep_ref, bf16[4,128,384]{2,1,0:T(8,128)(2,1)S(1)} %copy-done.1), custom_call_target="tpu_custom_call" | custom-call | tf_op jit(solution)/shard_map/pallas_call | solution.py:386
  109.5 0.4 convert_multiply_fusion
  109.9 0.3 fusion.1
  110.3 0.1 constant_dynamic-update-slice_fusion.2
  110.4 0.1 constant_dynamic-update-slice_fusion.1
  110.5 0.1 constant_dynamic-update-slice_fusion
  110.7 0.1 broadcast_dynamic-update-slice_fusion
  110.8 0.0 copy-start.3
  110.8 0.7 copy.11
  111.5 1.3 %copy.17 = bf16[4,128,384]{2,1,0:T(8,128)(2,1)} copy(bf16[4,128,384]{2,1,0:T(8,128)(2,1)S(1)} %get-tuple-element.13) | data formatting | bytes 786432
  112.7 1.1 copy-done.3
  (4 shorter events, 0.1 us)
Async XLA Ops:
  1.3 1.0 copy-start
  2.3 1.0 copy-start.1
  3.3 0.7 copy-start.2
  110.8 3.1 %copy-start.3 = (f32[12,384,384]{2,1,0:T(8,128)}, f32[12,384,384]{2,1,0:T(8,128)S(1)}, u32[]{:S(2)}) copy-start(f32[12,384,384]{2,1,0:T(8,128)S(1)} %broadcast_dynamic-update-slice_fusion) | copy-start | bytes 21233668

commit v3 on v2

--- a/solution.py
+++ b/solution.py
@@ -10,8 +10,9 @@
 MESH = pl.DeviceIdType.MESH
 F32 = jnp.float32
 BF16 = jnp.bfloat16
-UNITS = 4
-UNIT_ROWS = 1024
+UNITS = ((0, 1024), (1024, 512), (1536, 1024), (2560, 1536))
+SUM_ROWS = 4096
+BIAS_ROWS = 256
 
 
 def rows_times(a, b):
@@ -36,12 +37,12 @@
 
 
 def fused_kernel(
-    x_ref, w_ref, b_ref, keep_ref, cot_ref,
+    x_ref, w_hbm, b_ref, keep_ref, cot_ref,
     out_ref, sum_ref,
     edge0, act1, prev1, act2, turned2, turned_cot, turned_keep, act3, own_wide, turned_wide,
     slope, through, grad, grad2, up_out, up2, next1, edge_back,
-    acc, stage_send, stage_recv,
-    send_sem, recv_sem, sum_send_sem, sum_recv_sem,
+    acc, stage_send, stage_recv, w_ref,
+    send_sem, recv_sem, local_sem, sum_send_sem, sum_recv_sem,
 ):
     windows, frames, ch = x_ref.shape
     rows = windows * frames
@@ -64,19 +65,27 @@
     def at_z(other):
         return (y, other * 4 + cx)
 
-    partner = {
-        "core": (y, z * 4 + xx * 2 + (1 - core)),
-        "x": (y, z * 4 + (1 - xx) * 2 + core),
-        "y": (1 - y, thi),
-        "z1": at_z(near_z),
-        "z2": at_z(far_z),
+    plane = {
+        1: (1 - y, thi),
+        2: (y, z * 4 + (1 - xx) * 2 + core),
+        3: (1 - y, z * 4 + (1 - xx) * 2 + core),
     }
-    bit = {"core": core, "x": xx, "y": y, "z1": lax.rem(z, 2), "z2": z // 2}
-
+    plane_member = {
+        1: xx * 2 + (1 - y),
+        2: (1 - xx) * 2 + y,
+        3: (1 - xx) * 2 + (1 - y),
+    }
+    z_member = {1: near_z, 2: far_z, 3: 3 - z}
+    sibling = (y, z * 4 + xx * 2 + (1 - core))
+
+    load_w = pltpu.make_async_copy(w_hbm, w_ref, local_sem.at[0])
+    load_w.start()
+    load_cot = pltpu.make_async_copy(cot_ref.at[z], turned_cot.at[z], local_sem.at[1])
+    load_cot.start()
     barrier = pltpu.get_barrier_semaphore()
     greeted = [at_block(o) for o in (1, -1, 2, -2)]
     greeted += [at_z(other) for other in others]
-    greeted += [partner["core"], partner["x"], partner["y"]]
+    greeted += [sibling, plane[1], plane[2], plane[3]]
     for device in greeted:
         pl.semaphore_signal(barrier, inc=1, device_id=device, device_id_type=MESH)
 
@@ -106,13 +115,12 @@
         send(cot_ref.at[o], turned_cot.at[z], 43 + i, at_z(o)) for i, o in enumerate(others)
     ]
     turned_keep[z] = keep_ref[z]
-    turned_cot[z] = cot_ref[z]
     zeros = jnp.zeros((frames, ch), BF16)
     turned2[0] = zeros
     turned2[1] = zeros
     grad2[4] = zeros
     grad2[5] = zeros
-    acc[10 * ch :, :] = jnp.zeros((UNITS * UNIT_ROWS - 10 * ch, ch), F32)
+    acc[:BIAS_ROWS, :] = jnp.zeros((BIAS_ROWS, ch), F32)
     edge0[:, half:, :] = x_ref[...]
     bias = b_ref[...]
     across = lax.broadcasted_iota(jnp.int32, (frames, frames), 0) == lax.broadcasted_iota(
@@ -135,6 +143,8 @@
         total = rows_times_t(a, w_ref[level, 0]) + rows_times_t(b, w_ref[level, 1])
         return total + rows_times_t(c, w_ref[level, 2])
 
+    load_w.wait()
+    load_cot.wait()
     one_copies, two_copies = [], []
     for w, copy in zip(order, edge_copies):
         copy.wait_recv()
@@ -189,7 +199,7 @@
         ref[pl.ds(first, 2)] = value.reshape(2, frames, ch)
 
     def add_bias(level, g):
-        at = 10 * ch + 8 * level
+        at = 8 * level
         acc[at : at + 1, :] += jnp.sum(g.astype(F32), axis=0, keepdims=True)
 
     def far_levels(i, _):
@@ -224,37 +234,38 @@
             up2[z] = result.astype(BF16)
 
     def put_weight(slot, a, g):
-        acc[slot * ch : (slot + 1) * ch, :] = t_times_rows(a, g)
-
-    orders = (("x", "y", "z1", "z2"), ("y", "x", "z1", "z2"))
-
-    def plan(unit):
-        base = unit * UNIT_ROWS
-        size = UNIT_ROWS // 2
-        steps = [[("core", base + (1 - core) * size, base + core * size, size, base)]]
-        for _ in range(4):
-            steps.append([])
-        landing = base + size
-        for h, order in enumerate(orders):
-            at = base + core * size + h * (size // 2)
-            n = size // 2
-            for s, name in enumerate(order):
-                n = n // 2
-                steps[s + 1].append((name, at + (1 - bit[name]) * n, at + bit[name] * n, n, landing))
-                at = at + bit[name] * n
-                landing += n
-        return steps
-
-    plans = [plan(u) for u in range(UNITS)]
+        acc[BIAS_ROWS + slot * ch : BIAS_ROWS + (slot + 1) * ch, :] = t_times_rows(a, g)
+
+    def plan(base, size):
+        half_at = base + core * (size // 2)
+        n = size // 8
+        mine = xx * 2 + y
+        part = half_at + mine * n
+        first = [(sibling, base + (1 - core) * (size // 2), base)]
+        second = [
+            (plane[r], half_at + plane_member[r] * n, base + size // 2 + (r - 1) * n) for r in (1, 2, 3)
+        ]
+        m = size // 32
+        landed = base + size // 2 + 3 * n
+        third = [
+            (at_z(z_member[r]), part + z_member[r] * m, landed + (r - 1) * m) for r in (1, 2, 3)
+        ]
+        return (
+            (first, half_at, size // 2),
+            (second, part, n),
+            (third, part + z * m, m),
+        )
+
+    plans = [plan(*unit) for unit in UNITS]
     flying = {}
 
     def aligned(at, n):
         return pl.ds(at if isinstance(at, int) else pl.multiple_of(at, 16), n)
 
-    def sum_copy(src, dst, unit, index, name):
+    def sum_copy(src, dst, unit, index, device):
         copy = pltpu.make_async_remote_copy(
             src_ref=src, dst_ref=dst, send_sem=sum_send_sem.at[unit, index],
-            recv_sem=sum_recv_sem.at[unit, index], device_id=partner[name], device_id_type=MESH,
+            recv_sem=sum_recv_sem.at[unit, index], device_id=device, device_id_type=MESH,
         )
         copy.start()
         pending.append(copy)
@@ -262,32 +273,35 @@
 
     def begin(unit, stage):
         copies = []
-        if stage < 5:
-            for h, (name, give, _, n, landing) in enumerate(plans[unit][stage]):
-                stage_send[aligned(give, n), :] = acc[aligned(give, n), :].astype(BF16)
-                copies.append(sum_copy(
-                    stage_send.at[aligned(give, n), :], stage_recv.at[pl.ds(landing, n), :],
-                    unit, 2 * stage + h, name))
-        else:
-            for h, (name, _, own, n, _) in enumerate(plans[unit][9 - stage]):
-                span = aligned(own, n)
-                if stage == 5:
-                    sum_ref[span, :] = acc[span, :].astype(BF16)
-                copies.append(sum_copy(sum_ref.at[span, :], sum_ref.at[span, :], unit, 2 * stage + h, name))
+        routes, own, n = plans[unit][stage if stage < 3 else 5 - stage]
+        span = aligned(own, n)
+        if stage == 3:
+            sum_ref[span, :] = acc[span, :].astype(BF16)
+        for r, (device, give, landing) in enumerate(routes):
+            if stage < 3:
+                there = aligned(give, n)
+                stage_send[there, :] = acc[there, :].astype(BF16)
+                src, dst = stage_send.at[there, :], stage_recv.at[pl.ds(landing, n), :]
+            else:
+                src, dst = sum_ref.at[span, :], sum_ref.at[span, :]
+            copies.append(sum_copy(src, dst, unit, 3 * stage + r, device))
         flying[unit, stage] = copies
 
     def finish(unit, stage):
         for copy in flying[unit, stage]:
             copy.wait_recv()
-        if stage < 5:
-            for _, _, own, n, landing in plans[unit][stage]:
-                span = aligned(own, n)
-                acc[span, :] = acc[span, :] + stage_recv[landing : landing + n, :].astype(F32)
+        if stage < 3:
+            routes, own, n = plans[unit][stage]
+            span = aligned(own, n)
+            total = acc[span, :]
+            for _, _, landing in routes:
+                total = total + stage_recv[landing : landing + n, :].astype(F32)
+            acc[span, :] = total
 
     def advance(unit, stage):
         if stage > 0:
             finish(unit, stage - 1)
-        if stage < 10:
+        if stage < 6:
             begin(unit, stage)
 
     back_order = (z, near_z, far_z, 3 - z)
@@ -307,19 +321,20 @@
         add_bias(1, g)
 
     start_one(0)
-    put_weight(0, act3[...].reshape(rows, ch), grad[0].reshape(rows, ch))
+    put_weight(9, act3[...].reshape(rows, ch), grad[0].reshape(rows, ch))
     for tap in range(3):
         n = 4 - tap
-        put_weight(1 + tap, turned2[2 : 2 + n].reshape(n * frames, ch), grad2[tap:4].reshape(n * frames, ch))
+        put_weight(6 + tap, turned2[2 : 2 + n].reshape(n * frames, ch), grad2[tap:4].reshape(n * frames, ch))
+    advance(3, 0)
     for i in range(1, 4):
         start_one(i)
-    advance(0, 0)
+    advance(3, 1)
     g1 = grad[1].reshape(rows, ch)
-    put_weight(4, act1[...].reshape(rows, ch), g1)
-    put_weight(5, prev1[0].reshape(rows, ch), g1)
-    put_weight(6, prev1[1].reshape(rows, ch), g1)
-    advance(0, 1)
-    advance(1, 0)
+    put_weight(3, act1[...].reshape(rows, ch), g1)
+    put_weight(4, prev1[0].reshape(rows, ch), g1)
+    put_weight(5, prev1[1].reshape(rows, ch), g1)
+    advance(2, 0)
+    advance(3, 2)
     back_edges = []
     for i, w in enumerate(back_order):
         back_one[i].wait_recv()
@@ -343,18 +358,18 @@
             send(grad.at[2, w, :half, :], edge_back.at[w, frames:, :], 20 + w, at_block(-1))
         )
         add_bias(0, g)
-    advance(0, 2)
+    advance(2, 1)
+    advance(3, 3)
+    g0 = grad[2].reshape(rows, ch)
+    put_weight(0, x_ref[...].reshape(rows, ch), g0)
+    put_weight(1, edge0[:, quarter : quarter + frames].reshape(rows, ch), g0)
+    advance(0, 0)
+    put_weight(2, edge0[:, 0:frames].reshape(rows, ch), g0)
+    advance(1, 0)
+    advance(2, 2)
+    advance(0, 1)
     advance(1, 1)
-    g0 = grad[2].reshape(rows, ch)
-    put_weight(7, x_ref[...].reshape(rows, ch), g0)
-    advance(2, 0)
-    put_weight(8, edge0[:, quarter : quarter + frames].reshape(rows, ch), g0)
-    put_weight(9, edge0[:, 0:frames].reshape(rows, ch), g0)
-    advance(3, 0)
-    advance(0, 3)
-    advance(1, 2)
-    advance(2, 1)
-    advance(3, 1)
+    advance(3, 4)
     for i, w in enumerate(back_order):
         back_edges[i].wait_recv()
 
@@ -366,10 +381,10 @@
             0, grad[2, w], edge_back[w, quarter : quarter + frames], edge_back[w, half : half + frames]
         )
         out_ref[w] = total.astype(BF16)
-    at = [3, 2, 1, 1]
-    while min(at) < 10:
-        for u in range(UNITS):
-            if at[u] < 10:
+    at = [1, 1, 2, 4]
+    while min(at) < 6:
+        for u in range(len(UNITS)):
+            if at[u] < 6:
                 at[u] += 1
                 advance(u, at[u])
     for copy in pending:
@@ -381,15 +396,16 @@
     levels = weights.shape[0]
     keep = jnp.broadcast_to(valid_mask.astype(F32)[:, None, :], (windows, 8, frames))
     vmem = pl.BlockSpec(memory_space=pltpu.VMEM)
+    anywhere = pl.BlockSpec(memory_space=pl.ANY)
     block = (windows, frames, ch)
-    sum_rows = UNITS * UNIT_ROWS
+    sum_rows = SUM_ROWS
     grad_in, sums = pl.pallas_call(
         fused_kernel,
         out_shape=(
             jax.ShapeDtypeStruct(block, BF16),
             jax.ShapeDtypeStruct((sum_rows, ch), BF16),
         ),
-        in_specs=[vmem] * 5,
+        in_specs=[vmem, anywhere, vmem, vmem, anywhere],
         out_specs=(vmem, vmem),
         scratch_shapes=[
             pltpu.VMEM((windows, frames + frames // 2, ch), BF16),
@@ -413,10 +429,12 @@
             pltpu.VMEM((sum_rows, ch), F32),
             pltpu.VMEM((sum_rows, ch), BF16),
             pltpu.VMEM((sum_rows, ch), BF16),
+            pltpu.VMEM(weights.shape, BF16),
             pltpu.SemaphoreType.DMA((52,)),
             pltpu.SemaphoreType.DMA((52,)),
-            pltpu.SemaphoreType.DMA((UNITS, 20)),
-            pltpu.SemaphoreType.DMA((UNITS, 20)),
+            pltpu.SemaphoreType.DMA((2,)),
+            pltpu.SemaphoreType.DMA((len(UNITS), 18)),
+            pltpu.SemaphoreType.DMA((len(UNITS), 18)),
         ],
         compiler_params=pltpu.CompilerParams(
             collective_id=0, has_side_effects=True, vmem_limit_bytes=48 * 1024 * 1024
@@ -424,10 +442,8 @@
     )(frames_in, weights, biases, keep, cotangent)
     factor = 1.0 / math.sqrt(windows * frames * lax.axis_size("tlo") * lax.axis_size("thi"))
     scaled = sums.astype(F32) * factor
-    grads = scaled[: 10 * ch].reshape(10, ch, ch)
-    none = jnp.zeros((2, ch, ch), F32)
-    weight_grad = jnp.concatenate([grads[7:10], grads[4:7], grads[1:4], grads[0:1], none])
-    bias_grad = scaled[10 * ch : 10 * ch + 8 * levels].reshape(levels, 8, ch)[:, 0]
+    weight_grad = jnp.pad(scaled[BIAS_ROWS:], ((0, 2 * ch), (0, 0)))
+    bias_grad = scaled[: 8 * levels].reshape(levels, 8, ch)[:, 0]
     return (grad_in, weight_grad.reshape(levels, 3, ch, ch), bias_grad)
 
 

time: 114 us -> 109 us (0.956)
  Pallas kernels: 105 us -> 99.5 us
  local copies, waits for them, and re-layouts: 6.56 us -> 7.84 us
    pallas_call x1, Pallas kernels: 105 us -> 99.5 us  [fused_shards(): pl.pallas_call(fused_kernel, out_shape=(jax.ShapeDtypeStruct(block, BF16)...]
    pad x0 -> x1, local copies, waits for them, and re-layouts: none -> 3.42 us  [fused_shards(): weight_grad = jnp.pad(scaled[BIAS_ROWS:], ((0, 2 * ch), (0, 0)))]
    unnamed x14 -> x8, local copies, waits for them, and re-layouts: 6.12 us -> 4.02 us
where the time goes in v3:
time: 109 us
  Pallas kernels  99.5 us (91%)
  local copies, waits for them, and re-layouts  7.84 us (7%)
  other arithmetic  1.09 us (1%)
    pallas_call x1, Pallas kernels, fused_shards(): pl.pallas_call(fused_kernel, out_shape=(jax.ShapeDtypeStruct(block, BF16)...  99.5 us
    unnamed x8, local copies, waits for them, and re-layouts  4.02 us
    pad x1, local copies, waits for them, and re-layouts, fused_shards(): weight_grad = jnp.pad(scaled[BIAS_ROWS:], ((0, 2 * ch), (0, 0)))  3.42 us

profile of v3, /device:TPU:1, one launch (start us, length us, event | category | flops | bytes accessed | tf_op | source)
XLA Modules:
  0.0 109.1 jit_solution(404153902856945039)
XLA Ops:
  0.6 0.7 convert_element_type.8
  1.3 0.0 copy-start
  1.3 1.0 copy-done
  2.3 0.0 copy-start.1
  2.3 1.0 copy-done.1
  3.3 0.0 copy-start.2
  3.3 0.7 copy-done.2
  4.0 99.5 %shard_map.76 = (bf16[4,128,384]{2,1,0:T(8,128)(2,1)S(1)}, bf16[4096,384]{1,0:T(8,128)(2,1)S(1)}) custom-call(bf16[4,128,384]{2,1,0:T(8,128)(2,1)S(1)} %copy-done, bf16[4,3,384,384]{3,2,1,0:T(8,128)(2,1)} %w_hbm.1, f32[4,384]{1,0:T(4,128)S(1)} %copy-done.2, f32[4,8,128]{2,1,0:T(8,128)S(1)} %broadcast_in_dim.2.keep_ref, bf16[4,128,384]{2,1,0:T(8,128)(2,1)S(1)} %copy-done.1), custom_call_target="tpu_custom_call" | custom-call | tf_op jit(solution)/shard_map/pallas_call | solution.py:402
  103.5 0.4 convert_multiply_fusion
  103.9 0.4 slice.12
  104.3 0.6 copy.11
  104.9 3.4 %pad.4 = f32[4608,384]{1,0:T(8,128)} pad(f32[3840,384]{1,0:T(8,128)S(1)} %slice.12, f32[]{:T(128)} %constant.4.clone.1), padding=0_768x0_0 | pad | bytes 12976132 | tf_op jit(solution)/shard_map/jit(_pad)/pad | solution.py:445
  108.3 0.7 copy.13
  (3 shorter events, 0.0 us)
Async XLA Ops:
  1.3 1.0 copy-start
  2.3 1.0 copy-start.1
  3.3 0.7 copy-start.2

commit v4 on v3

--- a/solution.py
+++ b/solution.py
@@ -442,7 +442,9 @@
     )(frames_in, weights, biases, keep, cotangent)
     factor = 1.0 / math.sqrt(windows * frames * lax.axis_size("tlo") * lax.axis_size("thi"))
     scaled = sums.astype(F32) * factor
-    weight_grad = jnp.pad(scaled[BIAS_ROWS:], ((0, 2 * ch), (0, 0)))
+    none = jnp.zeros((2, ch, ch), F32)
+    grads = scaled[BIAS_ROWS:].reshape(10, ch, ch)
+    weight_grad = jnp.concatenate([grads[0:3], grads[3:6], grads[6:9], grads[9:10], none])
     bias_grad = scaled[: 8 * levels].reshape(levels, 8, ch)[:, 0]
     return (grad_in, weight_grad.reshape(levels, 3, ch, ch), bias_grad)
 

time: 109 us -> 108 us (level)
  local copies, waits for them, and re-layouts: 7.84 us -> 6.56 us
    pad x1 -> x0, local copies, waits for them, and re-layouts: 3.42 us -> none  [fused_shards(): weight_grad = jnp.pad(scaled[BIAS_ROWS:], ((0, 2 * ch), (0, 0)))]
    unnamed x8 -> x14, local copies, waits for them, and re-layouts: 4.02 us -> 6.12 us
where the time goes in v4:
time: 108 us
  Pallas kernels  99.5 us (92%)
  local copies, waits for them, and re-layouts  6.56 us (6%)
  other arithmetic  1.09 us (1%)
    pallas_call x1, Pallas kernels, fused_shards(): pl.pallas_call(fused_kernel, out_shape=(jax.ShapeDtypeStruct(block, BF16)...  99.5 us
    unnamed x14, local copies, waits for them, and re-layouts  6.12 us

profile of v4, /device:TPU:1, one launch (start us, length us, event | category | flops | bytes accessed | tf_op | source)
XLA Modules:
  0.0 107.9 jit_solution(13864776487693376280)
XLA Ops:
  0.6 0.7 convert_element_type.6
  1.3 0.0 copy-start
  1.3 1.0 copy-done
  2.3 0.0 copy-start.1
  2.3 1.0 copy-done.1
  3.3 0.0 copy-start.2
  3.3 0.7 copy-done.2
  4.0 99.5 %shard_map.76 = (bf16[4,128,384]{2,1,0:T(8,128)(2,1)S(1)}, bf16[4096,384]{1,0:T(8,128)(2,1)S(1)}) custom-call(bf16[4,128,384]{2,1,0:T(8,128)(2,1)S(1)} %copy-done, bf16[4,3,384,384]{3,2,1,0:T(8,128)(2,1)} %w_hbm.1, f32[4,384]{1,0:T(4,128)S(1)} %copy-done.2, f32[4,8,128]{2,1,0:T(8,128)S(1)} %broadcast_in_dim.4.keep_ref, bf16[4,128,384]{2,1,0:T(8,128)(2,1)S(1)} %copy-done.1), custom_call_target="tpu_custom_call" | custom-call | tf_op jit(solution)/shard_map/pallas_call | solution.py:402
  103.5 0.4 convert_multiply_fusion
  103.9 0.3 fusion.1
  104.3 0.1 constant_dynamic-update-slice_fusion.2
  104.4 0.1 constant_dynamic-update-slice_fusion.1
  104.5 0.1 constant_dynamic-update-slice_fusion
  104.7 0.1 broadcast_dynamic-update-slice_fusion
  104.8 0.0 copy-start.3
  104.8 0.7 copy.11
  105.5 1.3 %copy.17 = bf16[4,128,384]{2,1,0:T(8,128)(2,1)} copy(bf16[4,128,384]{2,1,0:T(8,128)(2,1)S(1)} %get-tuple-element.13) | data formatting | bytes 786432
  106.7 1.1 %copy-done.3 = f32[12,384,384]{2,1,0:T(8,128)} copy-done((f32[12,384,384]{2,1,0:T(8,128)}, f32[12,384,384]{2,1,0:T(8,128)S(1)}, u32[]{:S(2)}) %copy-start.3) | copy-done | bytes 7077912
  (4 shorter events, 0.1 us)
Async XLA Ops:
  1.3 1.0 copy-start
  2.3 1.0 copy-start.1
  3.3 0.7 copy-start.2
  104.8 3.1 %copy-start.3 = (f32[12,384,384]{2,1,0:T(8,128)}, f32[12,384,384]{2,1,0:T(8,128)S(1)}, u32[]{:S(2)}) copy-start(f32[12,384,384]{2,1,0:T(8,128)S(1)} %broadcast_dynamic-update-slice_fusion) | copy-start | bytes 21233668
